TPU v7x, 512 devices: a whole 4x8x8 slice. The times are simulated.
512 devices in a mesh: tm: 16 (over y, core), rows: 32 (over z, x).
Axes of the slice: x: 4, y: 8, z: 8, core: 2. Of those that a mesh axis runs over, the one named last changes fastest.
Arguments:
- features: float32 [32, 128, 128, 256], P('tm', 'rows'), may hold values from -60 to 60
- norm_gain: float32 [256], replicated, may hold values from 0.1 to 1.9
- conv_weight: float32 [3, 256, 256], replicated, may hold values from -0.21875 to 0.21875
- proj_weight: float32 [2048, 512], P(None, 'rows'), may hold values from -0.125 to 0.125
- attn_gain: float32 [512], replicated, may hold values from 0.5 to 6
- qkv_weight: float32 [512, 1536], P(None, 'rows'), may hold values from -0.25 to 0.25
- out_weight: float32 [512, 512], replicated, may hold values from -0.25 to 0.25
Outputs:
- encoded: float32 [16, 64, 64, 512], P('tm', 'rows')
All inputs are finite; a program needn't handle non-finite values.
Results may differ from a plain program's by a relative error of at most 0.0003.
Values sent between devices are 32-bit elements; how exact they have to be, the bound alone decides.
A program may use at most 128 MiB of HBM per device.

v0:
```python
import math

import jax
import jax.numpy as jnp
import numpy as np
from jax import lax
from jax.sharding import PartitionSpec as P

D = 512
GROUPS = 32


epsilon = 1e-06
highest = lax.Precision.HIGHEST


def prefix(shard, axis, combine, identity):
    length, index = (lax.axis_size(axis), lax.axis_index(axis))
    everything = lax.all_gather(shard, axis)
    start = jnp.broadcast_to(jnp.asarray(identity, shard.dtype), shard.shape)

    def lap(k, before):
        reached = k < index
        new = combine(before, everything[k])
        return jnp.where(reached, new, before)

    return lax.fori_loop(0, length, lap, start)


def from_behind(shard, axis, by):
    length = lax.axis_size(axis)
    pairs = [(i, i + by) for i in range(length) if 0 <= i + by < length]
    return lax.ppermute(shard, axis, pairs)


def hadamard_table():
    signs = np.ones((8, 8), np.float32)
    for source in range(8):
        for target in range(8):
            common = source & target
            parity = ((common & 1) + (common >> 1 & 1) + (common >> 2 & 1)) % 2
            signs[source, target] = 1.0 - 2.0 * parity
    return signs / np.sqrt(8.0)


def row_totals(partial_sums):
    return lax.psum(partial_sums, "rows")


def group_sums(values):
    frames_now = values.shape[0]
    channels = values.shape[-1]
    grouped = values.reshape(frames_now, -1, GROUPS, channels // GROUPS)
    return jnp.stack(
        [jnp.sum(grouped, axis=(1, 3)), jnp.sum(grouped * grouped, axis=(1, 3))], axis=-1
    )


def normalize(values, means, variance, gain):
    frames_now = values.shape[0]
    channels = values.shape[-1]
    grouped = values.reshape(frames_now, -1, GROUPS, channels // GROUPS)
    normed = (grouped - means[:, None, :, None]) * lax.rsqrt(variance + epsilon)[:, None, :, None]
    return normed.reshape(values.shape) * gain


def shards(features, norm_gain, conv_weight, proj_weight, attn_gain, qkv_weight, out_weight):
    frames, height, columns, channels = features.shape
    rows_count = lax.axis_size("rows")
    per_group = channels // GROUPS
    per_frame = row_totals(group_sums(features))
    slab_sums = jnp.sum(per_frame, axis=0)
    before = prefix(slab_sums, "tm", jnp.add, jnp.zeros_like(slab_sums))
    running = before[None] + jnp.cumsum(per_frame, axis=0)
    positions = lax.axis_index("tm") * frames + jnp.arange(frames, dtype=jnp.int32) + 1
    counts = positions.astype(jnp.float32) * float(height * rows_count * columns * per_group)
    means = running[..., 0] / counts[:, None]
    variance = running[..., 1] / counts[:, None] - means * means
    activated = jax.nn.silu(normalize(features, means, variance, norm_gain))
    prior = from_behind(activated, "tm", 1)
    padded = jnp.concatenate([prior, activated], axis=0).reshape(
        frames + 2, height * columns, channels
    )
    convolved = jnp.zeros((frames, height * columns, channels), jnp.float32)
    for lagged in range(3):
        convolved = convolved + jnp.einsum(
            "fmc,cd->fmd",
            padded[2 - lagged : 2 - lagged + frames],
            conv_weight[lagged],
            precision=highest,
        )
    residual = features + convolved.reshape(features.shape)
    half_f, half_h, half_w = (frames // 2, height // 2, columns // 2)
    local_count = half_h * half_w
    cell_stack = (
        residual.reshape(half_f, 2, half_h, 2, half_w, 2, channels)
        .transpose(0, 2, 4, 1, 3, 5, 6)
        .reshape(-1, 8, channels)
    )
    subbands = jnp.einsum(
        "jk,nkc->njc", jnp.asarray(hadamard_table()), cell_stack, precision=highest
    ).reshape(-1, 8 * channels)
    proj_full, qkv_full = (
        lax.all_gather(proj_weight, "rows", axis=1, tiled=True),
        lax.all_gather(qkv_weight, "rows", axis=1, tiled=True),
    )
    tokens = jnp.dot(subbands, proj_full, precision=highest)
    tokens = tokens.reshape(half_f, local_count, D)
    token_sums = row_totals(group_sums(tokens))
    token_count = float(rows_count * local_count * (D // GROUPS))
    token_means = token_sums[..., 0] / token_count
    token_variance = token_sums[..., 1] / token_count - token_means * token_means
    normed = normalize(tokens, token_means, token_variance, attn_gain)
    source = normed.reshape(-1, D)
    projected = jnp.dot(source, qkv_full, precision=highest)
    projected = projected.reshape(half_f, -1, 3 * D)
    score_scale = 1.0 / math.sqrt(float(D))
    queries = projected[..., :D]
    keys_local = projected[..., D : 2 * D]
    values_local = projected[..., 2 * D :]
    all_keys, all_values = (
        lax.all_gather(keys_local, "rows", axis=1, tiled=True),
        lax.all_gather(values_local, "rows", axis=1, tiled=True),
    )
    scores = jnp.einsum("fqd,fkd->fqk", queries, all_keys, precision=highest) * score_scale
    attended = jnp.einsum(
        "fqk,fkd->fqd", jax.nn.softmax(scores, axis=-1), all_values, precision=highest
    )
    encoded = tokens + jnp.einsum("fqd,de->fqe", attended, out_weight, precision=highest)
    return encoded.reshape(half_f, half_h, half_w, D)


def solution(mesh):
    in_specs = (P("tm", "rows", None, None), P(), P(), P(None, "rows"), P(), P(None, "rows"), P())
    out_specs = P("tm", "rows", None, None)
    return jax.shard_map(shards, mesh=mesh, in_specs=in_specs, out_specs=out_specs, check_vma=False)
```

profile of v0, /device:TPU:6, one launch (start us, length us, event | category | flops | bytes accessed | tf_op | source)
XLA Modules:
  0.0 432.9 jit_solution(18009817247135186210)
XLA Ops:
  6.5 0.7 all-gather.7.cloned.1.call-update
  7.3 0.7 all-gather.9.cloned.1.call-update
  8.1 1.4 fusion.27
  9.8 73.2 %psum.14 = f32[2,32,2]{1,0,2:T(2,128)S(1)} all-reduce(f32[2,32,2]{1,0,2:T(2,128)S(1)} %pad_maximum_fusion.1), channel_id=1, replica_groups=mesh['tm'=16,'rows'=32] {'rows'}, use_global_device_ids=true, to_apply=%region_4.5 | all-reduce | flops 128 | bytes 1024 | tf_op jit(solution)/shard_map/psum | solution.py:47
  83.0 17.5 %all-gather.1 = f32[16,32,2]{1,2,0:T(2,128)S(1)} all-gather(f32[1,32,2]{1,2,0:T(2,128)S(1)} %bitcast.88), channel_id=2, replica_groups=mesh['tm'=16,'rows'=32] {'tm'}, dimensions={0}, use_global_device_ids=true | all-gather | bytes 4352 | tf_op jit(solution)/shard_map/all_gather | solution.py:19
  100.5 0.6 while.14
  101.5 1.5 divide_multiply_fusion
  103.0 2.3 collective-permute-start
  105.3 1.0 fusion.13
  106.3 1.2 collective-permute-done
  107.6 1.0 convolution_add_fusion.1
  108.6 1.0 convolution_add_fusion
  109.6 0.1 add.106
  109.8 0.6 reshape.190
  110.4 0.4 copy.11
  110.8 0.7 reshape.191
  111.5 1.0 fusion.32
  112.5 0.3 copy.12
  112.9 6.6 %fusion.28 = (f32[512]{0:T(512)S(1)}, f32[512]{0:T(512)S(1)}, f32[128,512]{1,0:T(8,128)S(1)}) fusion(f32[128,2048]{1,0:T(8,128)S(1)} %bitcast.87, f32[2048,512]{0,1:T(8,128)} %all-gather.7.cloned.1.call-done), kind=kOutput, calls=%fused_computation.47 | convolution fusion | flops 1610808320 | bytes 5509120 | tf_op jit(solution)/shard_map/dot_general | solution.py:107
  119.6 0.1 reduce_sum.91
  119.8 0.1 reduce_sum.94
  119.9 75.0 %psum.15 = f32[1,32,2]{1,2,0:T(2,128)S(1)} all-reduce(f32[1,32,2]{1,2,0:T(2,128)S(1)} %pad_maximum_fusion.2), channel_id=1, replica_groups=mesh['tm'=16,'rows'=32] {'rows'}, use_global_device_ids=true, to_apply=%region_13.14 | all-reduce | flops 64 | bytes 512 | tf_op jit(solution)/shard_map/psum | solution.py:47
  195.3 5.1 %convolution_bitcast_fusion = f32[1,128,1536]{2,1,0:T(8,128)S(1)} fusion(f32[512,1536]{0,1:T(8,128)} %all-gather.9.cloned.1.call-done, f32[128,512]{1,0:T(8,128)S(1)} %get-tuple-element.116, f32[512]{0:T(512)S(1)} %copy-done.5, f32[512]{0:T(512)S(1)} %mul.106, f32[512]{0:T(512)S(1)} %sub.59), kind=kOutput, calls=%fused_computation.6 | convolution fusion | flops 1208156160 | bytes 4200448 | tf_op jit(solution)/shard_map/dot_general | solution.py:115
  200.5 0.9 copy-done.2
  201.4 0.8 fusion.30
  202.3 0.5 all-gather.13.cloned.1.call-update
  202.8 110.8 %all-gather.11.cloned.1.call-done = f32[1,4096,512]{2,1,0:T(8,128)} async-done(((f32[1,128,512]{2,1,0:T(8,128)}), f32[1,4096,512]{2,1,0:T(8,128)}) %all-gather.11.cloned.1.call-update) | async-done | bytes 8388624 | tf_op jit(solution)/shard_map/all_gather | solution.py:122
  313.5 11.1 %fusion.31 = (f32[128]{0:T(128)S(1)}, f32[128,4096]{1,0:T(8,128)S(1)}) fusion(f32[1,4096,512]{2,1,0:T(8,128)} %all-gather.11.cloned.1.call-done, f32[1,128,1536]{2,1,0:T(8,128)} %copy-done.2), kind=kOutput, calls=%fused_computation.49 | convolution fusion | flops 3222274048 | bytes 10748416 | tf_op jit(solution)/shard_map/fqd,fkd->fqk/dot_general | solution.py:125
  324.7 0.4 fusion.8
  325.1 92.6 %all-gather.13.cloned.1.call-done = f32[1,4096,512]{2,1,0:T(8,128)} async-done(((f32[1,128,512]{2,1,0:T(8,128)}), f32[1,4096,512]{2,1,0:T(8,128)}) %all-gather.13.cloned.1.call-update) | async-done | bytes 8388624 | tf_op jit(solution)/shard_map/all_gather | solution.py:123
  417.7 7.2 %fusion = f32[128,512]{1,0:T(8,128)S(1)} fusion(f32[1,4096,512]{2,1,0:T(8,128)} %all-gather.13.cloned.1.call-done, f32[128,4096]{1,0:T(8,128)S(1)} %get-tuple-element.118, f32[128]{0:T(128)S(1)} %fusion.8, f32[128]{0:T(128)S(1)} %get-tuple-element.117), kind=kOutput, calls=%fused_computation.1 | convolution fusion | flops 3222274048 | bytes 10748928 | tf_op jit(solution)/shard_map/fqk,fkd->fqd/dot_general | solution.py:126
  425.0 1.4 convolution_add_fusion.2
  (59 shorter events, 1.8 us)
Async XLA Ops:
  6.5 418.4 %copy-start = (f32[512,512]{1,0:T(8,128)S(1)}, f32[512,512]{1,0:T(8,128)}, u32[]{:S(2)}) copy-start(f32[512,512]{1,0:T(8,128)} %param.16) | copy-start | bytes 3145732
  6.5 98.8 %copy-start.3 = (f32[3,256,256]{2,1,0:T(8,128)S(1)}, f32[3,256,256]{2,1,0:T(8,128)}, u32[]{:S(2)}) copy-start(f32[3,256,256]{2,1,0:T(8,128)} %param.12) | copy-start | bytes 2359300
  6.5 106.4 %all-gather.7.cloned.1.call-start = ((), (), s32[]{:S(2)}) async-start(), calls=%async_computation | async-start | bytes 4325376 | tf_op jit(solution)/shard_map/all_gather | solution.py:104
  7.3 188.0 %all-gather.9.cloned.1.call-start = ((), (), s32[]{:S(2)}) async-start(), calls=%async_computation.1 | async-start | bytes 3244032 | tf_op jit(solution)/shard_map/all_gather | solution.py:105
  8.0 305.5 %all-gather.11.cloned.1.call-start = ((), (), s32[]{:S(2)}) async-start(), calls=%async_computation.2 | async-start | bytes 8650752 | tf_op jit(solution)/shard_map/all_gather | solution.py:122
  103.0 4.5 %collective-permute-start = (f32[2,4,128,256]{3,2,1,0:T(8,128)S(1)}, f32[2,4,128,256]{3,2,1,0:T(8,128)S(1)}, u32[]{:S(2)}, u32[]{:S(2)}) collective-permute-start(f32[2,4,128,256]{3,2,1,0:T(8,128)S(1)} %divide_multiply_fusion), channel_id=1, source_target_pairs={{0,32},{32,64},{64,96},{96,128},{128,160},{160,192},{192,224},{224... | collective-permute-start | bytes 3145736 | tf_op jit(solution)/shard_map/ppermute | solution.py:33
  107.6 2.0 copy-start.1
  109.8 1.7 copy-start.4
  112.9 82.4 %copy-start.5 = (f32[512]{0:T(512)S(1)}, f32[512]{0:T(512)}, u32[]{:S(2)}) copy-start(f32[512]{0:T(512)} %param.14) | copy-start | bytes 6148
  200.5 0.9 copy-start.2
  202.2 215.5 %all-gather.13.cloned.1.call-start = ((), (), s32[]{:S(2)}) async-start(), calls=%async_computation.3 | async-start | bytes 8650752 | tf_op jit(solution)/shard_map/all_gather | solution.py:123
Sparse Core Ops, SparseCore 0:
  10.5 91.0 all-gather.6
  104.8 83.0 all-gather.8
  202.3 111.1 all-gather.10
  316.6 101.1 all-gather.12
where the time goes:
time: 436 us; the launch traced here: 433 us
  waiting for transfers between devices  207 us (47%)
  blocking collectives  166 us (38%)
  matrix products  35.5 us (8%)
  between operations  13.4 us (3%)
  local copies, waits for them, and re-layouts  4.76 us (1%)
    psum x2, blocking collectives, row_totals(): return lax.psum(partial_sums, 'rows')  148 us
    all_gather x1, waiting for transfers between devices, shards(): lax.all_gather(keys_local, 'rows', axis=1, tiled=True)  111 us
    all_gather x1, waiting for transfers between devices, shards(): lax.all_gather(values_local, 'rows', axis=1, tiled=True)  92.6 us
    all_gather x1, blocking collectives, prefix(): everything = lax.all_gather(shard, axis)  17.5 us
    dot_general x1, matrix products, shards(): jnp.einsum('fqd,fkd->fqk', queries, all_keys, precision=highest)  11.1 us
  transfers between devices with their start and end apart: 5, of which 3 were waited for; matrix products, arithmetic and copies ran while one was open for 7% of the time, Pallas kernels for 0%

commit v1 on v0

v1 whole, which is shorter than its diff:
```python
import functools
import math

import jax
import jax.numpy as jnp
from jax import lax
from jax.experimental import pallas as pl
from jax.experimental.pallas import tpu as pltpu
from jax.sharding import PartitionSpec as P

GROUPS = 32
X = 4
epsilon = 1e-06
highest = lax.Precision.HIGHEST
f32, bf16 = jnp.float32, jnp.bfloat16
NN = (((1,), (0,)), ((), ()))
NT = (((1,), (1,)), ((), ()))
BOTH = (0, 1)


def split(value):
    high = value.astype(bf16)
    return high, (value - high.astype(f32)).astype(bf16)


def dot(a, b, dims):
    return lax.dot_general(a, b, dims, preferred_element_type=f32)


def dot3(a, b, dims=NN):
    rows = a[0].shape[0]
    if rows > 256:
        deep = (b[0], b[0], b[1])
        return dot(jnp.concatenate((a[0], a[1], a[0]), axis=1), jnp.concatenate(deep, axis=dims[0][1][0]), dims)
    by_high = dot(jnp.concatenate(a, axis=0), b[0], dims)
    return by_high[:rows] + (by_high[rows:] + dot(a[0], b[1], dims))


def exact(a, b):
    return lax.dot_general(a, b, NN, precision=highest, preferred_element_type=f32)


def iota(shape, axis):
    return lax.broadcasted_iota(jnp.int32, shape, axis)


def rsqrt(value):
    return lax.rsqrt(value + epsilon)


def mod(value, size):
    return lax.rem(value + size, size)


class Plan:
    def __init__(self):
        self.now, self.waits = 0.0, []

    def expect(self, time, name, action):
        self.waits.append((time, len(self.waits), name, action))

    def upto(self, time):
        while True:
            due = [wait for wait in self.waits if wait[0] <= time]
            if not due:
                return
            first = min(due, key=lambda wait: wait[:2])
            self.waits.remove(first)
            first[3]()

    def need(self, name):
        times = [wait[0] for wait in self.waits if wait[2] == name]
        if times:
            self.now = max(self.now, max(times))
            self.upto(max(times))

    def run(self, duration, action, *needs):
        for name in needs:
            self.need(name)
        self.upto(self.now)
        result = action()
        self.now += duration
        return result


class Links:
    def __init__(self, z_count, x_count, tm_count):
        self.rows, self.tm = lax.axis_index("rows"), lax.axis_index("tm")
        self.z, self.x = lax.div(self.rows, x_count), lax.rem(self.rows, x_count)
        self.y, self.core = lax.div(self.tm, 2), lax.rem(self.tm, 2)
        self.z_count, self.x_count, self.y_count = z_count, x_count, tm_count // 2

    def z_device(self, by):
        return {"rows": mod(self.z + by, self.z_count) * self.x_count + self.x}

    def x_device(self, by):
        return {"rows": self.z * self.x_count + mod(self.x + by, self.x_count)}

    def y_device(self, by):
        return {"tm": mod(self.y + by, self.y_count) * 2 + self.core}

    def sibling(self):
        return {"tm": self.tm + 1 - 2 * self.core}


def copy(src, dst, send, recv, device):
    return pltpu.make_async_remote_copy(
        src_ref=src, dst_ref=dst, send_sem=send, recv_sem=recv, device_id=device,
        device_id_type=pl.DeviceIdType.MESH,
    )


class Ring:
    def __init__(self, place, count, device, at, send, recv, reach, chunks=1, half=None, arrived=None):
        self.place, self.count, self.device, self.at, self.half = place, count, device, at, half
        self.send, self.recv, self.reach, self.chunks, self.arrived = send, recv, reach, chunks, arrived

    def moves(self, step, way, chunk):
        if step > self.reach[way]:
            return False
        shared = step == self.reach[0] == self.reach[1] and 2 * step == self.count
        return not shared or self.chunks == 1 or chunk == way

    def ref(self, away, step, way, chunk):
        ref = self.at(mod(self.place + away, self.count), chunk)
        return self.half(ref, way) if self.half and 2 * step == self.count else ref

    def copy(self, step, way, chunk, away):
        ref = self.ref(away, step, way, chunk)
        at = (way * self.chunks + chunk, step - 1)
        return copy(ref, ref, self.send.at[at], self.recv.at[at], self.device(1 if way == 0 else -1))

    def outgoing(self, step, way, chunk):
        return self.copy(step, way, chunk, 1 - step if way == 0 else step - 1)

    def start(self, way, chunk):
        self.outgoing(1, way, chunk).start()

    def step(self, step, way, chunk):
        if not self.moves(step, way, chunk):
            return
        away = -step if way == 0 else step
        self.copy(step, way, chunk, away).wait_recv()
        if self.moves(step + 1, way, chunk):
            self.outgoing(step + 1, way, chunk).start()
        if self.arrived:
            self.arrived(self.ref(away, step, way, chunk))

    def each(self):
        for step in range(1, max(self.reach) + 1):
            for chunk in range(self.chunks):
                for way in BOTH:
                    if self.moves(step, way, chunk):
                        yield step, way, chunk

    def finish(self):
        for step, way, chunk in self.each():
            self.outgoing(step, way, chunk).wait_send()


class Sums:
    def __init__(self, slots, index, per, size, device, send, recv):
        self.slots, self.index, self.per, self.size, self.device = slots, index, per, size, device
        self.send, self.recv = send, recv

    def copies(self, by):
        ref = self.slots.at[pl.ds(self.index * self.per, self.per)]
        return copy(ref, ref, self.send, self.recv, self.device(by))

    def everything(self):
        ref = self.slots.at[pl.ds(0, (self.size - 1) * self.per)]
        return copy(ref, ref, self.send, self.recv, self.device(1))

    def start(self):
        for by in range(1, self.size):
            self.copies(by).start()

    def wait(self):
        self.everything().wait_recv()

    def finish(self):
        self.everything().wait_send()


class Proj:
    def __init__(self, links, buf, sems):
        self.k, self.buf = links, buf
        az_s, az_r, self.ax_s, self.ax_r, self.bx_s, self.bx_r, bz_s, bz_r, self.c_s, self.c_r = sems
        self.core = links.core
        rows, xs, steps = buf.shape[4] // 2, links.x_count // 2, links.z_count // 2
        self.first = Ring(links.z, links.z_count, links.z_device, lambda z, chunk: buf.at[self.core, 0, z, links.x],
                          az_s, az_r, (steps, steps), 1, lambda ref, way: ref.at[pl.ds(way * rows, rows)])
        self.second = Ring(links.z, links.z_count, links.z_device,
                           lambda z, chunk: buf.at[self.core, 1, z, pl.ds(chunk * xs, xs)],
                           bz_s, bz_r, (steps, steps), 2, None, self.hand_second)
        self.steps = steps

    def ax(self, away, by):
        ref = self.buf.at[self.core, 0, mod(self.k.z + away, self.k.z_count), self.k.x]
        return copy(ref, ref, self.ax_s.at[by], self.ax_r.at[by], self.k.x_device(by))

    def ax_all(self, by, away):
        ref = self.buf.at[self.core, 0, :, mod(self.k.x + away, self.k.x_count)]
        return copy(ref, ref, self.ax_s.at[by], self.ax_r.at[by], self.k.x_device(by))

    def bx(self, by, away):
        ref = self.buf.at[self.core, 1, self.k.z, mod(self.k.x + away, self.k.x_count)]
        return copy(ref, ref, self.bx_s.at[by], self.bx_r.at[by], self.k.x_device(by))

    def hand(self, part, ref):
        return copy(ref, ref, self.c_s.at[part], self.c_r.at[part], self.k.sibling())

    def hand_second(self, ref):
        self.hand(1, ref).start()

    def start(self):
        for by in range(1, self.k.x_count):
            self.bx(by, 0).start()
        for way in BOTH:
            self.first.start(way, 0)
        for by in range(1, self.k.x_count):
            self.ax(0, by).start()

    def a_step(self, n):
        for way in BOTH:
            self.first.step(n, way, 0)
        for away in (-n, n) if n < self.steps else (n,):
            for by in range(1, self.k.x_count):
                self.ax(away, by).start()

    def b_start(self):
        for by in range(1, self.k.x_count):
            self.bx(by, -by).wait_recv()
        for chunk in range(2):
            for way in BOTH:
                self.second.start(way, chunk)
        self.hand(1, self.buf.at[self.core, 1, self.k.z]).start()

    def b_step(self, n, chunk):
        for way in BOTH:
            self.second.step(n, way, chunk)

    def a_swap(self):
        for by in range(self.k.x_count):
            if by:
                self.ax_all(by, -by).wait_recv()
            self.hand(0, self.buf.at[self.core, 0, :, mod(self.k.x - by, self.k.x_count)]).start()

    def wait(self, part):
        self.hand(part, self.buf.at[1 - self.core, part]).wait_recv()

    def finish(self):
        self.first.finish()
        self.second.finish()
        for by in range(1, self.k.x_count):
            self.ax_all(by, 0).wait_send()
            self.bx(by, 0).wait_send()
        for part in range(2):
            self.hand(part, self.buf.at[self.core, part]).wait_send()


class Qkv:
    def __init__(self, links, piece, buf, sems):
        self.k, self.buf, self.source = links, buf, piece
        self.load_s, self.x_s, self.x_r, self.z_s, self.z_r, e_s, e_r, l_s, l_r, self.c_s, self.c_r = sems
        self.zs, self.xs = buf.shape[2], buf.shape[3]
        self.early = early = self.zs * 3 // 4
        up = (links.y_count - 1) // 3
        reach = (up, links.y_count - 1 - up)
        half = self.xs // 2
        mine = lambda y, *rest: buf.at[(links.core, y, *rest)]
        self.first = Ring(links.y, links.y_count, links.y_device,
                          lambda y, c: mine(y, pl.ds(0, early), pl.ds(c * half, half)),
                          e_s, e_r, reach, 2, None, lambda ref: self.hand(0, ref).start())
        self.last = Ring(links.y, links.y_count, links.y_device, lambda y, c: mine(y, pl.ds(early, self.zs - early)),
                         l_s, l_r, reach, 1, None, lambda ref: self.hand(1, ref).start())
        self.sends = lax.rem(links.z, 2) == links.core
        self.zz = lax.div(links.z, 2)

    def load(self):
        return pltpu.make_async_copy(self.source, self.buf.at[self.k.core, self.k.y, self.zz, self.k.x], self.load_s.at[0])

    def preload(self):
        pl.when(self.sends)(lambda: self.load().start())

    def z_copy(self, by):
        ref = self.buf.at[self.k.core, self.k.y, self.zz, self.k.x]
        return copy(ref, ref, self.z_s.at[0], self.z_r.at[0], self.k.z_device(by))

    def x_copy(self, by):
        ref = self.buf.at[self.k.core, self.k.y, :, self.k.x]
        return copy(ref, ref, self.x_s.at[0], self.x_r.at[0], self.k.x_device(by))

    def x_all(self):
        ref = self.buf.at[self.k.core, self.k.y, :, pl.ds(0, self.xs - 1)]
        return copy(ref, ref, self.x_s.at[0], self.x_r.at[0], self.k.x_device(1))

    def start(self):
        @pl.when(self.sends)
        def _():
            self.load().wait()
            for by in range(1, self.k.z_count):
                self.z_copy(by).start()

    def across(self):
        def got(count):
            ref = self.buf.at[self.k.core, self.k.y, pl.ds(0, count), self.k.x]
            copy(ref, ref, self.z_s.at[0], self.z_r.at[0], self.k.z_device(1)).wait_recv()

        pl.when(self.sends)(lambda: got(self.zs - 1))
        pl.when(jnp.logical_not(self.sends))(lambda: got(self.zs))
        for by in range(1, self.xs):
            self.x_copy(by).start()

    def collect(self):
        self.x_all().wait_recv()
        for chunk in range(2):
            self.first.start(1, chunk)
        for part in range(2):
            self.hand(part, self.part_of(part, self.k.core, self.k.y)).start()

    def up(self):
        for chunk in range(2):
            self.first.start(0, chunk)

    def rest(self):
        for way in BOTH:
            self.last.start(way, 0)

    def hand(self, part, ref):
        return copy(ref, ref, self.c_s.at[part], self.c_r.at[part], self.k.sibling())

    def part_of(self, part, core, y):
        zs = pl.ds(0, self.early) if part == 0 else pl.ds(self.early, self.zs - self.early)
        return self.buf.at[core, y, zs]

    def all_of(self, part, core):
        return self.hand(part, self.part_of(part, core, slice(None)))

    def wait(self, part):
        self.all_of(part, 1 - self.k.core).wait_recv()

    def finish(self):
        self.first.finish()
        self.last.finish()
        for part in range(2):
            self.all_of(part, self.k.core).wait_send()

        self.x_all().wait_send()

        @pl.when(self.sends)
        def _():
            ref = self.buf.at[self.k.core, pl.ds(0, self.k.z_count - 1), 0, self.k.x]
            copy(ref, ref, self.z_s.at[0], self.z_r.at[0], self.k.z_device(1)).wait_send()


def kernel(
    z_count, tm_count,
    features, gain, conv, proj, attn_gain, qkv, out_weight, out,
    feat, halo, conv_in, out_in, x_sums, z_sums, slab_sums, token_x, token_z,
    proj_all, qkv_all, act_hi, act_lo, residual, band_hi, band_lo, tokens, keys, queries, q_hi, q_lo, total, top, mass,
    partial, lse_mine, parts, lse_parts,
    load_s, halo_s, halo_r, sum_s, sum_r, *sems,
):
    proj_sems, qkv_sems, sems = sems[:10], sems[10:21], sems[21:]
    key_s, key_r, query_s, query_r, part_s, part_r, lse_s, lse_r = sems
    k = Links(z_count, X, tm_count)
    rows_count = z_count * X
    tm, z, x = k.tm, k.z, k.x
    frames, height, columns, channels = features.shape
    half_w = columns // 2
    count = (height // 2) * half_w
    width = tokens.shape[1]
    wide = proj_all.shape[5]
    per_half, narrow = qkv_all.shape[4:]
    steps = z_count // 2
    plan = Plan()

    loads = [
        pltpu.make_async_copy(features.at[:, :, :, pl.ds(128 * half, 128)], feat.at[half], load_s.at[half])
        for half in range(2)
    ]
    for load in loads:
        load.start()
    barrier = pltpu.get_barrier_semaphore()
    peers = (
        [k.x_device(by) for by in range(1, X)] + [k.z_device(by) for by in range(1, z_count)]
        + [k.y_device(by) for by in range(1, k.y_count)] + [k.sibling(), {"tm": mod(tm - 1 + 2 * k.core, tm_count)}]
    )
    for peer in peers:
        pl.semaphore_signal(barrier, inc=1, device_id=peer, device_id_type=pl.DeviceIdType.MESH)

    quarters = [
        pltpu.make_async_copy(
            proj.at[:, pl.ds(pl.multiple_of((2 * k.core + part) * wide, wide), wide)],
            proj_all.at[k.core, part, z, x], load_s.at[2 + part],
        )
        for part in range(2)
    ]
    piece = qkv.at[
        pl.ds(pl.multiple_of(lax.div(k.y, 4) * per_half, 8), per_half),
        pl.ds(pl.multiple_of(lax.rem(k.y, 4) * narrow, narrow), narrow),
    ]
    proj_w = Proj(k, proj_all, proj_sems)
    qkv_w = Qkv(k, piece, qkv_all, qkv_sems)
    for one in quarters:
        one.start()
    qkv_w.preload()
    weight_loads = [
        pltpu.make_async_copy(conv, conv_in, load_s.at[4]), pltpu.make_async_copy(out_weight, out_in, load_s.at[5])
    ]
    for one in weight_loads:
        one.start()

    lane = iota((8, 128), 1)
    row = iota((8, 128), 0)
    sums = []
    for load in loads:
        load.wait()
    for frame in range(frames):
        values = jnp.concatenate([feat[half, frame].reshape(height * columns, 128) for half in range(2)], axis=1)
        sums += [jnp.sum(values, axis=0, keepdims=True), jnp.sum(values * values, axis=0, keepdims=True)]
    stacked = jnp.concatenate(sums + [jnp.zeros((4, channels), f32)], axis=0)
    per_group = channels // GROUPS
    fold = (iota((channels, 128), 1) % GROUPS == iota((channels, 128), 0) // per_group).astype(f32)

    def lanes_of(rows_of_sums, table):
        return jnp.sum(jnp.where(lane // GROUPS == row, exact(rows_of_sums, table), 0.0), axis=0, keepdims=True)

    x_sums[x] = lanes_of(stacked, fold)
    for one in quarters:
        one.wait()

    def exchange(slots, index, per, size, device, n):
        return Sums(slots, index, per, size, device, sum_s.at[n], sum_r.at[n])

    over_x = exchange(x_sums, x, 1, X, k.x_device, 0)
    over_z = exchange(z_sums, z, 1, z_count, k.z_device, 1)
    over_y = exchange(slab_sums, k.y, 2, k.y_count, k.y_device, 2)
    tokens_x = exchange(token_x, x, 1, X, k.x_device, 3)
    tokens_z = exchange(token_z, z, 1, z_count, k.z_device, 4)

    def slab_copy(at):
        return copy(slab_sums.at[at], slab_sums.at[at], sum_s.at[5], sum_r.at[5], k.sibling())

    pl.semaphore_wait(barrier, len(peers))
    over_x.start()
    proj_w.start()
    halo_copies = [
        copy(feat.at[:, f], halo.at[:, f], halo_s.at[f], halo_r.at[f], {"tm": mod(tm + 1, tm_count)}) for f in range(frames)
    ]
    for one in halo_copies:
        one.start()
    qkv_w.start()
    plan.now = 6.0

    def summed_x():
        over_x.wait()
        z_sums[z] = jnp.sum(x_sums[...], axis=0)
        over_z.start()

    def summed_z():
        over_z.wait()
        slab_sums[tm] = jnp.sum(z_sums[...], axis=0)
        slab_copy(tm).start()

    def summed_core():
        slab_copy(tm + 1 - 2 * k.core).wait_recv()
        over_y.start()

    plan.expect(7.5, "x", summed_x)
    plan.expect(9.2, "qkv x", qkv_w.across)
    plan.expect(8.5, "b", proj_w.b_start)
    for n in range(1, steps + 1):
        plan.expect(6.0 + 2.2 * n, "a", functools.partial(proj_w.a_step, n))
        for chunk in range(2):
            plan.expect(9.0 + 1.9 * (2 * n - 1 + chunk), "b", functools.partial(proj_w.b_step, n, chunk))
    plan.expect(9.8, "z", summed_z)
    plan.expect(11.5, "core", summed_core)
    plan.expect(11.8, "collect", qkv_w.collect)
    plan.expect(14.5, "y", over_y.wait)
    for frame in range(frames):
        plan.expect(19.0 + 0.1 * frame, "halo", halo_copies[frame].wait_recv)
    plan.expect(19.2, "up", qkv_w.up)
    qkv_done = 14.5
    for step, way, chunk in qkv_w.first.each():
        time = (13.5 if way else 20.0) + 1.8 * (2 * step - 1 + chunk)
        qkv_done = max(qkv_done, time)
        plan.expect(time, "qkv", functools.partial(qkv_w.first.step, step, way, chunk))
    plan.expect(qkv_done + 0.1, "rest", qkv_w.rest)
    plan.expect(qkv_done + 1.0, "qkv", functools.partial(qkv_w.wait, 0))
    for step, way, chunk in qkv_w.last.each():
        plan.expect(qkv_done + 4.0 + 2.5 * step, "qkv last", functools.partial(qkv_w.last.step, step, way, chunk))
    plan.expect(qkv_done + 6.0 + 2.5 * max(qkv_w.last.reach), "qkv last", functools.partial(qkv_w.wait, 1))

    def split_taps():
        weight_loads[0].wait()
        return [split(conv_in[lag]) for lag in range(3)]

    taps = plan.run(0.4, split_taps)

    def statistics():
        everything = slab_sums[...]
        slab = iota(everything.shape, 0)
        earlier = jnp.sum(jnp.where(slab < tm - 1, everything, 0.0), axis=0)
        previous = jnp.sum(jnp.where(slab == tm - 1, everything, 0.0), axis=0)
        own = jnp.sum(jnp.where(slab == tm, everything, 0.0), axis=0)
        kind, upto = row % 2, row // 2
        lane_kind, lane_frame = lane // GROUPS % 2, lane // GROUPS // 2
        mine = lane_kind == kind
        running = (
            jnp.where(mine, earlier, 0.0)
            + jnp.where(mine & (lane_frame <= upto), previous, 0.0)
            + jnp.where(mine & (lane_frame <= upto - 2), own, 0.0)
        )
        unfold = (iota((128, channels), 0) % GROUPS == iota((128, channels), 1) // per_group).astype(f32)
        running = exact(running, unfold)
        means, scales = [], []
        for i in range(4):
            position = jnp.maximum(tm * frames + i - 1, 1).astype(f32)
            cells = position * float(rows_count * height * columns * per_group)
            mean = running[2 * i : 2 * i + 1] / cells
            variance = running[2 * i + 1 : 2 * i + 2] / cells - mean * mean
            means.append(mean)
            scales.append(rsqrt(variance))
        return means, scales

    means, scales = plan.run(0.6, statistics, "y")
    norm_gain = gain[...]

    def cells_of(src, frame, b, c):
        return jnp.concatenate([
            jnp.concatenate([src[half, frame, 2 * h + b, pl.ds(c, half_w, stride=2), :] for half in range(2)], axis=1)
            for h in range(height // 2)
        ], axis=0)

    def activate(src, frame, at):
        for b in range(2):
            for c in range(2):
                value = (cells_of(src, frame, b, c) - means[at]) * scales[at] * norm_gain
                value = value / (1.0 + jnp.exp(-value))
                if at < 2:
                    value = jnp.where(tm > 0, value, 0.0)
                high, low = split(value)
                place = pl.ds((2 * b + c) * count, count)
                act_hi[at, place] = high
                act_lo[at, place] = low

    def activated(at):
        return act_hi[at], act_lo[at]

    def convolve(frame, terms, first=False):
        value = functools.reduce(jnp.add, [dot3(activated(at), taps[lag]) for at, lag in terms])
        residual[frame] = value if first else residual[frame] + value

    plan.run(0.7, lambda: activate(feat, 0, 2))
    plan.run(0.7, lambda: activate(feat, 1, 3))
    plan.run(0.5, lambda: convolve(0, [(2, 0)], True))
    plan.run(1.0, lambda: convolve(1, [(3, 0), (2, 1)], True))
    plan.run(0.7, lambda: activate(halo, 0, 0), "halo")
    plan.run(0.7, lambda: activate(halo, 1, 1))
    plan.run(1.0, lambda: convolve(0, [(1, 1), (0, 2)]))
    plan.run(0.5, lambda: convolve(1, [(1, 2)]))

    def haar():
        bands = [
            residual[a, pl.ds((2 * b + c) * count, count)] + cells_of(feat, a, b, c)
            for a in range(2) for b in range(2) for c in range(2)
        ]
        for bit in (4, 2, 1):
            bands = [
                bands[j] + bands[j | bit] if not j & bit else bands[j ^ bit] - bands[j] for j in range(8)
            ]
        bands = [split(band * (1.0 / math.sqrt(8.0))) for band in bands]
        per_quarter = wide // channels
        for quarter in range(4):
            ours = bands[quarter * per_quarter : (quarter + 1) * per_quarter]
            band_hi[quarter] = jnp.concatenate([band[0] for band in ours], axis=1)
            band_lo[quarter] = jnp.concatenate([band[1] for band in ours], axis=1)

    plan.run(0.7, haar)

    def quarter_of(half, part):
        at = 2 * half + part
        return dot3((band_hi[at], band_lo[at]), split(proj_all[half, part].reshape(width, wide)), NT)

    plan.need("a")
    plan.run(0.3, proj_w.a_swap)
    made = plan.run(0.7, lambda: quarter_of(k.core, 0))
    made = made + plan.run(0.7, lambda: quarter_of(k.core, 1), "b")
    proj_w.wait(0)
    made = made + plan.run(0.7, lambda: quarter_of(1 - k.core, 0))
    proj_w.wait(1)
    made = made + plan.run(0.7, lambda: quarter_of(1 - k.core, 1))
    tokens[...] = made
    keys[z] = made
    queries[x] = made

    part_rows = count // 2
    key_ring = Ring(z, z_count, k.z_device, lambda at, c: keys.at[at, pl.ds(c * part_rows, part_rows)],
                    key_s, key_r, (steps, steps), 2)
    query_ring = Ring(x, X, k.x_device, lambda at, c: queries.at[at], query_s, query_r, (X // 2, X // 2), 1,
                      lambda ref, way: ref.at[pl.ds(way * part_rows, part_rows)])
    for way in BOTH:
        query_ring.start(way, 0)
    for chunk in range(2):
        for way in BOTH:
            key_ring.start(way, chunk)
    begin = plan.now
    for step, way, chunk in key_ring.each():
        plan.expect(begin + 1.5 + 2.9 * (2 * step - 1 + chunk) - (2.9 * chunk if step == steps else 0.0), f"key{step}",
                    functools.partial(key_ring.step, step, way, chunk))
    for step, way, chunk in query_ring.each():
        plan.expect(begin + 4.4 * step + 3.0, "queries", functools.partial(query_ring.step, step, way, chunk))

    token_group = width // GROUPS
    sums = jnp.concatenate(
        [jnp.sum(made, axis=0, keepdims=True), jnp.sum(made * made, axis=0, keepdims=True), jnp.zeros((6, width), f32)],
        axis=0,
    )
    fold = (iota((width, 128), 1) % GROUPS == iota((width, 128), 0) // token_group).astype(f32)
    token_x[x] = lanes_of(sums, fold)
    tokens_x.start()

    def token_summed_x():
        tokens_x.wait()
        token_z[z] = jnp.sum(token_x[...], axis=0)
        tokens_z.start()

    plan.expect(begin + 2.5, "tokens x", token_summed_x)
    plan.expect(begin + 5.0, "tokens z", tokens_z.wait)

    def token_statistics():
        all_sums = jnp.sum(token_z[...], axis=0)
        unfold = (iota((128, width), 0) % GROUPS == iota((128, width), 1) // token_group).astype(f32)
        spread_sums = exact(jnp.where(lane // GROUPS == row, all_sums, 0.0), unfold)
        token_count = float(rows_count * count * token_group)
        mean = spread_sums[0:1] / token_count
        return mean, rsqrt(spread_sums[1:2] / token_count - mean * mean)

    token_mean, token_scale = plan.run(0.6, token_statistics, "tokens z")
    token_gain = attn_gain[...]

    def normed(value):
        return split((value - token_mean) * token_scale * token_gain)

    def columns_of(block):
        lanes = []
        for lane_at in range(4):
            chunks = []
            for at in range(block * width // per_half, (block + 1) * width // per_half + 1):
                owner, part = at // 2, at % 2
                if owner < rows_count:
                    own_z, own_x = owner // X, owner % X
                    chunks.append(qkv_all[own_z % 2, 4 * part + lane_at, own_z // 2, own_x])
            skip = block * width - block * width // per_half * per_half
            lanes.append(jnp.concatenate(chunks, axis=0)[skip : skip + width])
        return split(jnp.concatenate(lanes, axis=1))

    def query_key_weight():
        query_weight = tuple(jnp.transpose(part.astype(f32)).astype(bf16) for part in columns_of(0))
        return split(dot3(query_weight, columns_of(1)) * (1.0 / math.sqrt(float(width))))

    def ask():
        high, low = split(dot3(normed(queries[...].reshape(X * count, width)), query_key))
        q_hi[...], q_lo[...] = high.reshape(q_hi.shape), low.reshape(q_lo.shape)

    query_key = plan.run(2.0, query_key_weight, "qkv")
    plan.run(1.5, ask, "queries")

    sets = [(0, -1, 1)] + [(-step, step) for step in range(2, steps)] + [(steps,)]

    def key_block(at):
        return normed(jnp.concatenate([keys[mod(z + away, z_count)] for away in sets[at]], axis=0))

    def attend(step, at, block):
        rows_of = lambda ref: ref[at].reshape(-1, ref.shape[-1])
        scores = dot3((rows_of(q_hi), rows_of(q_lo)), block, NT)
        here = jnp.max(scores, axis=1, keepdims=True)
        if step == 0:
            new_top = here
            weights = jnp.exp(scores - new_top)
            new_mass = jnp.sum(weights, axis=1, keepdims=True)
            value = dot3(split(weights), block)
        else:
            new_top = jnp.maximum(rows_of(top), here)
            fade = jnp.exp(rows_of(top) - new_top)
            weights = jnp.exp(scores - new_top)
            new_mass = rows_of(mass) * fade + jnp.sum(weights, axis=1, keepdims=True)
            value = rows_of(total) * fade + dot3(split(weights), block)
        return new_top, new_mass, value

    def attend_all(step):
        for ref, value in zip((top, mass, total), attend(step, slice(None), key_block(step))):
            ref[...] = value.reshape(ref.shape)

    for step in range(len(sets) - 1):
        plan.run(3.0 if step == 0 else 2.2, lambda: attend_all(step), f"key{step + 1}")

    def part_copy(by, at):
        return copy(partial.at[mod(x + by, X)], parts.at[at], part_s.at[by], part_r.at[by], k.x_device(by))

    def lse_copy(by, at):
        return copy(lse_mine.at[mod(x + by, X)], lse_parts.at[at], lse_s.at[by], lse_r.at[by], k.x_device(by))

    plan.need(f"key{steps}")
    block = key_block(-1)
    for by in (2, 1, 3, 0):
        at = mod(x + by, X)
        last_top, last_mass, value = attend(steps, pl.ds(at, 1), block)
        partial[at] = value / last_mass
        lse_mine[at] = jnp.transpose(jnp.broadcast_to(last_top + jnp.log(last_mass), (count, 128)))[0:1]
        if by:
            lse_copy(by, x).start()
            part_copy(by, x).start()
        else:
            parts[x] = partial[x]
            lse_parts[x] = lse_mine[x]
    plan.now += 1.5

    def value_to_out():
        weight_loads[1].wait()
        value_weight = columns_of(2)
        value_weight = tuple(jnp.transpose(part.astype(f32)).astype(bf16) for part in value_weight)
        return split(dot3(value_weight, split(out_in[...])))

    value_out = plan.run(2.0, value_to_out, "qkv last")
    plan.upto(1e9)
    proj_w.finish()
    qkv_w.finish()
    for one in halo_copies:
        one.wait_send()
    for one in (over_x, over_z, over_y, tokens_x, tokens_z):
        one.finish()
    slab_copy(tm).wait_send()
    key_ring.finish()
    query_ring.finish()
    for by in range(1, X):
        lse_copy(by, mod(x - by, X)).wait_recv()
    for by in (1, 3, 2):
        part_copy(by, mod(x - by, X)).wait_recv()
    shares = [lse_parts[at] for at in range(X)]
    highest_lse = functools.reduce(jnp.maximum, shares)
    shares = [jnp.exp(share - highest_lse) for share in shares]
    whole = functools.reduce(jnp.add, shares)
    merged = jnp.zeros((count, width), f32)
    for at in range(X):
        share = jnp.transpose(jnp.broadcast_to(shares[at] / whole, (128, count)))
        merged = merged + parts[at] * jnp.concatenate([share] * (width // 128), axis=1)
    encoded = tokens[...] + dot3(split(merged), value_out)
    out[...] = encoded.reshape(out.shape)

    for by in range(1, X):
        part_copy(by, x).wait_send()
        lse_copy(by, x).wait_send()


def shards(z_count, tm_count, features, norm_gain, conv_weight, proj_weight, attn_gain, qkv_weight, out_weight):
    frames, height, columns, channels = features.shape
    width = out_weight.shape[0]
    half_h, half_w = height // 2, columns // 2
    count = half_h * half_w
    steps = z_count // 2
    rows_count = z_count * X
    proj_rows, qkv_rows = proj_weight.shape[1], qkv_weight.shape[1] // 2
    wide, narrow = proj_weight.shape[0] // 4, qkv_weight.shape[0] // 4
    y_count = tm_count // 2
    far = y_count - 1 - (y_count - 1) // 3
    vmem = pltpu.VMEM
    dma = pltpu.SemaphoreType.DMA
    proj_sems = [dma((2, steps)), dma((2, steps)), dma((X,)), dma((X,)), dma((X,)), dma((X,)), dma((4, steps)),
                 dma((4, steps)), dma((2,)), dma((2,))]
    qkv_sems = [dma((1,)), dma((1,)), dma((1,)), dma((1,)), dma((1,)), dma((4, far)), dma((4, far)), dma((2, far)),
                dma((2, far)), dma((2,)), dma((2,))]
    scratch = [
        vmem((2, frames, height, columns, 128), f32), vmem((2, frames, height, columns, 128), f32),
        vmem(conv_weight.shape, f32), vmem(out_weight.shape, f32),
        vmem((X, 1, 128), f32), vmem((z_count, 1, 128), f32), vmem((tm_count, 1, 128), f32),
        vmem((X, 1, 128), f32), vmem((z_count, 1, 128), f32),
        vmem((2, 2, z_count, X, proj_rows, wide), f32),
        vmem((2, y_count, z_count // 2, X, qkv_rows, narrow), f32),
        vmem((4, 4 * count, channels), bf16), vmem((4, 4 * count, channels), bf16),
        vmem((frames, 4 * count, channels), f32),
        vmem((4, count, wide), bf16), vmem((4, count, wide), bf16),
        vmem((count, width), f32),
        vmem((z_count, count, width), f32),
        vmem((X, count, width), f32),
        vmem((X, count, width), bf16), vmem((X, count, width), bf16),
        vmem((X, count, width), f32), vmem((X, count, 1), f32), vmem((X, count, 1), f32),
        vmem((X, count, width), f32), vmem((X, 1, 128), f32),
        vmem((X, count, width), f32), vmem((X, 1, 128), f32),
        dma((6,)), dma((frames,)), dma((frames,)), dma((6,)), dma((6,)),
        *proj_sems, *qkv_sems,
        dma((4, steps)), dma((4, steps)), dma((2, X // 2)), dma((2, X // 2)), dma((X,)), dma((X,)), dma((X,)), dma((X,)),
    ]
    whole = pl.BlockSpec(memory_space=vmem)
    anywhere = pl.BlockSpec(memory_space=pl.ANY)
    return pl.pallas_call(
        functools.partial(kernel, z_count, tm_count),
        out_shape=jax.ShapeDtypeStruct((frames // 2, half_h, half_w, width), f32),
        in_specs=[anywhere, whole, anywhere, anywhere, whole, anywhere, anywhere],
        out_specs=whole,
        scratch_shapes=scratch,
        compiler_params=pltpu.CompilerParams(collective_id=0, has_side_effects=True, vmem_limit_bytes=56 * 2**20),
    )(features, norm_gain[None], conv_weight, proj_weight.T, attn_gain[None], qkv_weight.T, out_weight)


def solution(mesh):
    in_specs = (P("tm", "rows", None, None), P(), P(), P(None, "rows"), P(), P(None, "rows"), P())
    out_specs = P("tm", "rows", None, None)
    body = functools.partial(shards, mesh.shape["rows"] // X, mesh.shape["tm"])
    return jax.shard_map(body, mesh=mesh, in_specs=in_specs, out_specs=out_specs, check_vma=False)
```

time: 436 us -> 94.8 us (0.22)
  the two profiles are of different devices: /device:TPU:6 before, /device:TPU:9 now
where the time goes in v1:
time: 94.8 us; the launch traced here: 94.6 us
  Pallas kernels  93 us (98%)
  local copies, waits for them, and re-layouts  1.67 us (2%)
    pallas_call x1, Pallas kernels, shards(): pl.pallas_call(functools.partial(kernel, z_count, tm_count), out_shape=ja...  93 us

profile of v1, /device:TPU:9, one launch (start us, length us, event | category | flops | bytes accessed | tf_op | source)
XLA Modules:
  0.0 94.6 jit_solution(75606449634394267)
XLA Ops:
  0.0 93.0 %shard_map.73 = f32[1,2,64,512]{3,2,1,0:T(8,128)} custom-call(f32[2,4,128,256]{3,2,1,0:T(8,128)} %features.1, f32[1,256]{1,0:T(1,128)} %bitcast.7, f32[3,256,256]{2,1,0:T(8,128)} %conv.1, f32[16,2048]{1,0:T(8,128)} %bitcast.4, f32[1,512]{1,0:T(1,128)} %bitcast.6, f32[48,512]{1,0:T(8,128)} %bitcast.5, f32[512,512]{1,0:T(8,128)} %out_weight.1), custom_call_target="tpu_custom_call" | custom-call | tf_op jit(solution)/shard_map/pallas_call | solution.py:798
  93.0 1.7 %copy.9 = f32[1,2,64,512]{3,2,1,0:T(8,128)} copy(f32[1,2,64,512]{3,2,1,0:T(8,128)} %shard_map.73) | data formatting | bytes 524288

commit v2 on v1

--- a/solution.py
+++ b/solution.py
@@ -195,13 +195,29 @@
                            bz_s, bz_r, (steps, steps), 2, None, self.hand_second)
         self.steps = steps
 
-    def ax(self, away, by):
-        ref = self.buf.at[self.core, 0, mod(self.k.z + away, self.k.z_count), self.k.x]
-        return copy(ref, ref, self.ax_s.at[by], self.ax_r.at[by], self.k.x_device(by))
-
-    def ax_all(self, by, away):
-        ref = self.buf.at[self.core, 0, :, mod(self.k.x + away, self.k.x_count)]
-        return copy(ref, ref, self.ax_s.at[by], self.ax_r.at[by], self.k.x_device(by))
+    def block(self, away, x_away):
+        return self.buf.at[self.core, 0, mod(self.k.z + away, self.k.z_count), mod(self.k.x + x_away, self.k.x_count)]
+
+    def ax(self, kind, away, x_away):
+        ref = self.block(away, x_away)
+        up = self.goes_up(away) if kind == 2 else kind == 0
+        at = (kind, away % self.k.z_count)
+        return copy(ref, ref, self.ax_s.at[at], self.ax_r.at[at], self.k.x_device(1 if up else -1))
+
+    def goes_up(self, away):
+        return away % self.k.z_count < self.steps
+
+    def a_out(self, away):
+        for kind in range(2):
+            self.ax(kind, away, 0).start()
+
+    def a_on(self, away):
+        for kind, x_away in enumerate((-1, 1)):
+            self.ax(kind, away, x_away).wait_recv()
+        self.ax(2, away, -1 if self.goes_up(away) else 1).start()
+
+    def aways(self, n):
+        return (0,) if n == 0 else (-n, n) if n < self.steps else (n,)
 
     def bx(self, by, away):
         ref = self.buf.at[self.core, 1, self.k.z, mod(self.k.x + away, self.k.x_count)]
@@ -218,15 +234,17 @@
             self.bx(by, 0).start()
         for way in BOTH:
             self.first.start(way, 0)
-        for by in range(1, self.k.x_count):
-            self.ax(0, by).start()
+        self.a_out(0)
 
     def a_step(self, n):
         for way in BOTH:
             self.first.step(n, way, 0)
-        for away in (-n, n) if n < self.steps else (n,):
-            for by in range(1, self.k.x_count):
-                self.ax(away, by).start()
+        for away in self.aways(n):
+            self.a_out(away)
+
+    def a_pass(self, n):
+        for away in self.aways(n):
+            self.a_on(away)
 
     def b_start(self):
         for by in range(1, self.k.x_count):
@@ -240,11 +258,17 @@
         for way in BOTH:
             self.second.step(n, way, chunk)
 
-    def a_swap(self):
-        for by in range(self.k.x_count):
-            if by:
-                self.ax_all(by, -by).wait_recv()
-            self.hand(0, self.buf.at[self.core, 0, :, mod(self.k.x - by, self.k.x_count)]).start()
+    def a_hand(self, by):
+        self.hand(0, self.buf.at[self.core, 0, :, mod(self.k.x + by, self.k.x_count)]).start()
+
+    def a_near(self):
+        for by in (0, -1, 1):
+            self.a_hand(by)
+
+    def a_far(self):
+        for away in range(self.k.z_count):
+            self.ax(2, away, 2).wait_recv()
+        self.a_hand(2)
 
     def wait(self, part):
         self.hand(part, self.buf.at[1 - self.core, part]).wait_recv()
@@ -253,8 +277,10 @@
         self.first.finish()
         self.second.finish()
         for by in range(1, self.k.x_count):
-            self.ax_all(by, 0).wait_send()
             self.bx(by, 0).wait_send()
+        for away in range(self.k.z_count):
+            for kind in range(3):
+                self.ax(kind, away, 0).wait_send()
         for part in range(2):
             self.hand(part, self.buf.at[self.core, part]).wait_send()
 
@@ -359,11 +385,11 @@
     features, gain, conv, proj, attn_gain, qkv, out_weight, out,
     feat, halo, conv_in, out_in, x_sums, z_sums, slab_sums, token_x, token_z,
     proj_all, qkv_all, act_hi, act_lo, residual, band_hi, band_lo, tokens, keys, queries, q_hi, q_lo, total, top, mass,
-    partial, lse_mine, parts, lse_parts,
+    partial, lse_mine, relay, relay_lse, joint, joint_lse, parts, parts_lse,
     load_s, halo_s, halo_r, sum_s, sum_r, *sems,
 ):
     proj_sems, qkv_sems, sems = sems[:10], sems[10:21], sems[21:]
-    key_s, key_r, query_s, query_r, part_s, part_r, lse_s, lse_r = sems
+    key_s, key_r, query_s, query_r, part_s, part_r = sems
     k = Links(z_count, X, tm_count)
     rows_count = z_count * X
     tm, z, x = k.tm, k.z, k.x
@@ -445,12 +471,16 @@
 
     pl.semaphore_wait(barrier, len(peers))
     over_x.start()
-    proj_w.start()
-    halo_copies = [
-        copy(feat.at[:, f], halo.at[:, f], halo_s.at[f], halo_r.at[f], {"tm": mod(tm + 1, tm_count)}) for f in range(frames)
-    ]
+    pairs = height // 2
+
+    def halo_copy(f, h):
+        at = (slice(None), f, pl.ds(2 * h, 2))
+        return copy(feat.at[at], halo.at[at], halo_s.at[f, h], halo_r.at[f, h], {"tm": mod(tm + 1, tm_count)})
+
+    halo_copies = [halo_copy(f, h) for h in range(pairs) for f in range(frames)]
     for one in halo_copies:
         one.start()
+    proj_w.start()
     qkv_w.start()
     plan.now = 6.0
 
@@ -471,16 +501,21 @@
     plan.expect(7.5, "x", summed_x)
     plan.expect(9.2, "qkv x", qkv_w.across)
     plan.expect(8.5, "b", proj_w.b_start)
+    plan.expect(9.0, "a", functools.partial(proj_w.a_pass, 0))
+    plan.expect(8.9 + 2.4 * steps, "a", proj_w.a_near)
+    plan.expect(11.5 + 2.4 * steps, "a far", proj_w.a_far)
     for n in range(1, steps + 1):
-        plan.expect(6.0 + 2.2 * n, "a", functools.partial(proj_w.a_step, n))
+        plan.expect(6.0 + 2.4 * n, "a", functools.partial(proj_w.a_step, n))
+        plan.expect(8.8 + 2.4 * n, "a", functools.partial(proj_w.a_pass, n))
         for chunk in range(2):
             plan.expect(9.0 + 1.9 * (2 * n - 1 + chunk), "b", functools.partial(proj_w.b_step, n, chunk))
     plan.expect(9.8, "z", summed_z)
     plan.expect(11.5, "core", summed_core)
     plan.expect(11.8, "collect", qkv_w.collect)
     plan.expect(14.5, "y", over_y.wait)
-    for frame in range(frames):
-        plan.expect(19.0 + 0.1 * frame, "halo", halo_copies[frame].wait_recv)
+    for h in range(pairs):
+        for frame in range(frames):
+            plan.expect(13.5 + 5.8 * h + 0.1 * frame, f"halo{h}", halo_copy(frame, h).wait_recv)
     plan.expect(19.2, "up", qkv_w.up)
     qkv_done = 14.5
     for step, way, chunk in qkv_w.first.each():
@@ -528,43 +563,45 @@
     means, scales = plan.run(0.6, statistics, "y")
     norm_gain = gain[...]
 
-    def cells_of(src, frame, b, c):
-        return jnp.concatenate([
-            jnp.concatenate([src[half, frame, 2 * h + b, pl.ds(c, half_w, stride=2), :] for half in range(2)], axis=1)
-            for h in range(height // 2)
-        ], axis=0)
-
-    def activate(src, frame, at):
+    def cells_of(src, frame, h, b, c):
+        return jnp.concatenate([src[half, frame, 2 * h + b, pl.ds(c, half_w, stride=2), :] for half in range(2)], axis=1)
+
+    def activate(src, frame, h, at):
         for b in range(2):
             for c in range(2):
-                value = (cells_of(src, frame, b, c) - means[at]) * scales[at] * norm_gain
+                value = (cells_of(src, frame, h, b, c) - means[at]) * scales[at] * norm_gain
                 value = value / (1.0 + jnp.exp(-value))
                 if at < 2:
                     value = jnp.where(tm > 0, value, 0.0)
                 high, low = split(value)
-                place = pl.ds((2 * b + c) * count, count)
-                act_hi[at, place] = high
-                act_lo[at, place] = low
-
-    def activated(at):
-        return act_hi[at], act_lo[at]
-
-    def convolve(frame, terms, first=False):
-        value = functools.reduce(jnp.add, [dot3(activated(at), taps[lag]) for at, lag in terms])
-        residual[frame] = value if first else residual[frame] + value
-
-    plan.run(0.7, lambda: activate(feat, 0, 2))
-    plan.run(0.7, lambda: activate(feat, 1, 3))
-    plan.run(0.5, lambda: convolve(0, [(2, 0)], True))
-    plan.run(1.0, lambda: convolve(1, [(3, 0), (2, 1)], True))
-    plan.run(0.7, lambda: activate(halo, 0, 0), "halo")
-    plan.run(0.7, lambda: activate(halo, 1, 1))
-    plan.run(1.0, lambda: convolve(0, [(1, 1), (0, 2)]))
-    plan.run(0.5, lambda: convolve(1, [(1, 2)]))
+                place = pl.ds((2 * b + c) * half_w, half_w)
+                act_hi[at, h, place] = high
+                act_lo[at, h, place] = low
+
+    def activated(at, h):
+        return tuple(ref[at, h].reshape(-1, channels) for ref in (act_hi, act_lo))
+
+    def convolve(frame, h, terms, first=False):
+        value = functools.reduce(jnp.add, [dot3(activated(at, h), taps[lag]) for at, lag in terms])
+        value = value.reshape((-1, 4 * half_w, channels))
+        residual[frame, h] = value if first else residual[frame, h] + value
+
+    every = pl.ds(0, pairs)
+    for frame in range(frames):
+        plan.run(0.7, lambda: [activate(feat, frame, h, 2 + frame) for h in range(pairs)])
+    plan.run(0.5, lambda: convolve(0, every, [(2, 0)], True))
+    plan.run(1.0, lambda: convolve(1, every, [(3, 0), (2, 1)], True))
+    for h in range(pairs):
+        for frame in range(frames):
+            plan.run(0.35, lambda: activate(halo, frame, h, frame), f"halo{h}")
+        plan.run(0.6, lambda: convolve(0, pl.ds(h, 1), [(1, 1), (0, 2)]))
+        plan.run(0.3, lambda: convolve(1, pl.ds(h, 1), [(1, 2)]))
 
     def haar():
         bands = [
-            residual[a, pl.ds((2 * b + c) * count, count)] + cells_of(feat, a, b, c)
+            jnp.concatenate([
+                residual[a, h, pl.ds((2 * b + c) * half_w, half_w)] + cells_of(feat, a, h, b, c) for h in range(pairs)
+            ], axis=0)
             for a in range(2) for b in range(2) for c in range(2)
         ]
         for bit in (4, 2, 1):
@@ -584,9 +621,7 @@
         at = 2 * half + part
         return dot3((band_hi[at], band_lo[at]), split(proj_all[half, part].reshape(width, wide)), NT)
 
-    plan.need("a")
-    plan.run(0.3, proj_w.a_swap)
-    made = plan.run(0.7, lambda: quarter_of(k.core, 0))
+    made = plan.run(0.7, lambda: quarter_of(k.core, 0), "a far")
     made = made + plan.run(0.7, lambda: quarter_of(k.core, 1), "b")
     proj_w.wait(0)
     made = made + plan.run(0.7, lambda: quarter_of(1 - k.core, 0))
@@ -697,11 +732,28 @@
     for step in range(len(sets) - 1):
         plan.run(3.0 if step == 0 else 2.2, lambda: attend_all(step), f"key{step + 1}")
 
-    def part_copy(by, at):
-        return copy(partial.at[mod(x + by, X)], parts.at[at], part_s.at[by], part_r.at[by], k.x_device(by))
-
-    def lse_copy(by, at):
-        return copy(lse_mine.at[mod(x + by, X)], lse_parts.at[at], lse_s.at[by], lse_r.at[by], k.x_device(by))
+    half_rows = [pl.ds(way * part_rows, part_rows) for way in BOTH]
+    toward = (1, -1)
+
+    def send(kind, way, src, dst):
+        return copy(src, dst, part_s.at[kind, way], part_r.at[kind, way], k.x_device(toward[way]))
+
+    def opposite(way):
+        at = mod(x + 2, X)
+        return (send(0, way, partial.at[at, half_rows[way]], relay.at[way]),
+                send(1, way, lse_mine.at[at], relay_lse.at[way]))
+
+    def plain(way):
+        return (send(2, way, partial.at[mod(x + toward[way], X), half_rows[1 - way]], parts.at[way, half_rows[1 - way]]),)
+
+    def joined(way):
+        return (send(3, way, joint.at[way], parts.at[way, half_rows[way]]), send(4, way, joint_lse.at[way], parts_lse.at[way]))
+
+    def as_column(lanes):
+        return jnp.transpose(jnp.broadcast_to(lanes, (count, 128)))
+
+    def across(column):
+        return jnp.concatenate([column] * (width // 128), axis=1)
 
     plan.need(f"key{steps}")
     block = key_block(-1)
@@ -710,12 +762,11 @@
         last_top, last_mass, value = attend(steps, pl.ds(at, 1), block)
         partial[at] = value / last_mass
         lse_mine[at] = jnp.transpose(jnp.broadcast_to(last_top + jnp.log(last_mass), (count, 128)))[0:1]
-        if by:
-            lse_copy(by, x).start()
-            part_copy(by, x).start()
-        else:
-            parts[x] = partial[x]
-            lse_parts[x] = lse_mine[x]
+        if by == 2:
+            for one in (*opposite(0), *opposite(1)):
+                one.start()
+        elif by:
+            plain(0 if by == 1 else 1)[0].start()
     plan.now += 1.5
 
     def value_to_out():
@@ -726,6 +777,23 @@
 
     value_out = plan.run(2.0, value_to_out, "qkv last")
     plan.upto(1e9)
+    lane_row = iota((1, 128), 1)
+    for way in BOTH:
+        for one in opposite(way):
+            one.wait_recv()
+        at = mod(x + toward[way], X)
+        own, theirs = lse_mine[at], relay_lse[way]
+        both = jnp.maximum(own, theirs)
+        both = both + jnp.log(jnp.exp(own - both) + jnp.exp(theirs - both))
+        rows_of_way = slice(way * part_rows, (way + 1) * part_rows)
+        joint[way] = (
+            partial[at, half_rows[way]] * across(as_column(jnp.exp(own - both))[rows_of_way])
+            + relay[way] * across(as_column(jnp.exp(theirs - both))[rows_of_way])
+        )
+        joint_lse[way] = jnp.where(lane_row // part_rows == way, both, own)
+        for one in joined(way):
+            one.start()
+
     proj_w.finish()
     qkv_w.finish()
     for one in halo_copies:
@@ -735,24 +803,22 @@
     slab_copy(tm).wait_send()
     key_ring.finish()
     query_ring.finish()
-    for by in range(1, X):
-        lse_copy(by, mod(x - by, X)).wait_recv()
-    for by in (1, 3, 2):
-        part_copy(by, mod(x - by, X)).wait_recv()
-    shares = [lse_parts[at] for at in range(X)]
-    highest_lse = functools.reduce(jnp.maximum, shares)
-    shares = [jnp.exp(share - highest_lse) for share in shares]
+    for way in BOTH:
+        for one in (*plain(way), *joined(way)):
+            one.wait_recv()
+    given = [(lse_mine[x], partial[x])] + [(parts_lse[way], parts[way]) for way in BOTH]
+    highest_lse = functools.reduce(jnp.maximum, [lse for lse, _ in given])
+    shares = [jnp.exp(lse - highest_lse) for lse, _ in given]
     whole = functools.reduce(jnp.add, shares)
     merged = jnp.zeros((count, width), f32)
-    for at in range(X):
-        share = jnp.transpose(jnp.broadcast_to(shares[at] / whole, (128, count)))
-        merged = merged + parts[at] * jnp.concatenate([share] * (width // 128), axis=1)
+    for share, (_, value) in zip(shares, given):
+        merged = merged + value * across(as_column(share / whole))
     encoded = tokens[...] + dot3(split(merged), value_out)
     out[...] = encoded.reshape(out.shape)
 
-    for by in range(1, X):
-        part_copy(by, x).wait_send()
-        lse_copy(by, x).wait_send()
+    for way in BOTH:
+        for one in (*opposite(way), *plain(way), *joined(way)):
+            one.wait_send()
 
 
 def shards(z_count, tm_count, features, norm_gain, conv_weight, proj_weight, attn_gain, qkv_weight, out_weight):
@@ -768,7 +834,7 @@
     far = y_count - 1 - (y_count - 1) // 3
     vmem = pltpu.VMEM
     dma = pltpu.SemaphoreType.DMA
-    proj_sems = [dma((2, steps)), dma((2, steps)), dma((X,)), dma((X,)), dma((X,)), dma((X,)), dma((4, steps)),
+    proj_sems = [dma((2, steps)), dma((2, steps)), dma((3, z_count)), dma((3, z_count)), dma((X,)), dma((X,)), dma((4, steps)),
                  dma((4, steps)), dma((2,)), dma((2,))]
     qkv_sems = [dma((1,)), dma((1,)), dma((1,)), dma((1,)), dma((1,)), dma((4, far)), dma((4, far)), dma((2, far)),
                 dma((2, far)), dma((2,)), dma((2,))]
@@ -779,8 +845,8 @@
         vmem((X, 1, 128), f32), vmem((z_count, 1, 128), f32),
         vmem((2, 2, z_count, X, proj_rows, wide), f32),
         vmem((2, y_count, z_count // 2, X, qkv_rows, narrow), f32),
-        vmem((4, 4 * count, channels), bf16), vmem((4, 4 * count, channels), bf16),
-        vmem((frames, 4 * count, channels), f32),
+        vmem((4, half_h, 4 * half_w, channels), bf16), vmem((4, half_h, 4 * half_w, channels), bf16),
+        vmem((frames, half_h, 4 * half_w, channels), f32),
         vmem((4, count, wide), bf16), vmem((4, count, wide), bf16),
         vmem((count, width), f32),
         vmem((z_count, count, width), f32),
@@ -788,10 +854,12 @@
         vmem((X, count, width), bf16), vmem((X, count, width), bf16),
         vmem((X, count, width), f32), vmem((X, count, 1), f32), vmem((X, count, 1), f32),
         vmem((X, count, width), f32), vmem((X, 1, 128), f32),
-        vmem((X, count, width), f32), vmem((X, 1, 128), f32),
-        dma((6,)), dma((frames,)), dma((frames,)), dma((6,)), dma((6,)),
+        vmem((2, count // 2, width), f32), vmem((2, 1, 128), f32),
+        vmem((2, count // 2, width), f32), vmem((2, 1, 128), f32),
+        vmem((2, count, width), f32), vmem((2, 1, 128), f32),
+        dma((6,)), dma((frames, half_h)), dma((frames, half_h)), dma((6,)), dma((6,)),
         *proj_sems, *qkv_sems,
-        dma((4, steps)), dma((4, steps)), dma((2, X // 2)), dma((2, X // 2)), dma((X,)), dma((X,)), dma((X,)), dma((X,)),
+        dma((4, steps)), dma((4, steps)), dma((2, X // 2)), dma((2, X // 2)), dma((5, 2)), dma((5, 2)),
     ]
     whole = pl.BlockSpec(memory_space=vmem)
     anywhere = pl.BlockSpec(memory_space=pl.ANY)

time: 94.8 us -> 90.6 us (0.956)
  the two profiles are of different devices: /device:TPU:9 before, /device:TPU:6 now
where the time goes in v2:
time: 90.6 us; the launch traced here: 90.4 us
  Pallas kernels  88.7 us (98%)
  local copies, waits for them, and re-layouts  1.67 us (2%)
    pallas_call x1, Pallas kernels, shards(): pl.pallas_call(functools.partial(kernel, z_count, tm_count), out_shape=ja...  88.7 us

profile of v2, /device:TPU:6, one launch (start us, length us, event | category | flops | bytes accessed | tf_op | source)
XLA Modules:
  0.0 90.4 jit_solution(17700153835985749954)
XLA Ops:
  0.0 88.7 %shard_map.73 = f32[1,2,64,512]{3,2,1,0:T(8,128)} custom-call(f32[2,4,128,256]{3,2,1,0:T(8,128)} %features.1, f32[1,256]{1,0:T(1,128)} %bitcast.7, f32[3,256,256]{2,1,0:T(8,128)} %conv.1, f32[16,2048]{1,0:T(8,128)} %bitcast.4, f32[1,512]{1,0:T(1,128)} %bitcast.6, f32[48,512]{1,0:T(8,128)} %bitcast.5, f32[512,512]{1,0:T(8,128)} %out_weight.1), custom_call_target="tpu_custom_call" | custom-call | tf_op jit(solution)/shard_map/pallas_call | solution.py:866
  88.7 1.7 %copy.9 = f32[1,2,64,512]{3,2,1,0:T(8,128)} copy(f32[1,2,64,512]{3,2,1,0:T(8,128)} %shard_map.73) | data formatting | bytes 524288

commit v3 on v2

--- a/solution.py
+++ b/solution.py
@@ -119,7 +119,7 @@
         if step > self.reach[way]:
             return False
         shared = step == self.reach[0] == self.reach[1] and 2 * step == self.count
-        return not shared or self.chunks == 1 or chunk == way
+        return not shared or self.chunks == 1 or chunk // (self.chunks // 2) == way
 
     def ref(self, away, step, way, chunk):
         ref = self.at(mod(self.place + away, self.count), chunk)
@@ -384,7 +384,7 @@
     z_count, tm_count,
     features, gain, conv, proj, attn_gain, qkv, out_weight, out,
     feat, halo, conv_in, out_in, x_sums, z_sums, slab_sums, token_x, token_z,
-    proj_all, qkv_all, act_hi, act_lo, residual, band_hi, band_lo, tokens, keys, queries, q_hi, q_lo, total, top, mass,
+    proj_all, qkv_all, act_hi, act_lo, residual, band_hi, band_lo, proj_hi, proj_lo, tokens, keys, queries, q_hi, q_lo, total, top, mass,
     partial, lse_mine, relay, relay_lse, joint, joint_lse, parts, parts_lse,
     load_s, halo_s, halo_r, sum_s, sum_r, *sems,
 ):
@@ -482,7 +482,7 @@
         one.start()
     proj_w.start()
     qkv_w.start()
-    plan.now = 6.0
+    plan.now = 4.0
 
     def summed_x():
         over_x.wait()
@@ -498,35 +498,35 @@
         slab_copy(tm + 1 - 2 * k.core).wait_recv()
         over_y.start()
 
-    plan.expect(7.5, "x", summed_x)
-    plan.expect(9.2, "qkv x", qkv_w.across)
-    plan.expect(8.5, "b", proj_w.b_start)
-    plan.expect(9.0, "a", functools.partial(proj_w.a_pass, 0))
-    plan.expect(8.9 + 2.4 * steps, "a", proj_w.a_near)
-    plan.expect(11.5 + 2.4 * steps, "a far", proj_w.a_far)
+    plan.expect(6.3, "x", summed_x)
+    plan.expect(7.8, "qkv x", qkv_w.across)
+    plan.expect(6.8, "b", proj_w.b_start)
+    plan.expect(7.5, "a", functools.partial(proj_w.a_pass, 0))
     for n in range(1, steps + 1):
-        plan.expect(6.0 + 2.4 * n, "a", functools.partial(proj_w.a_step, n))
-        plan.expect(8.8 + 2.4 * n, "a", functools.partial(proj_w.a_pass, n))
+        plan.expect(4.0 + 2.7 * n, "a", functools.partial(proj_w.a_step, n))
+        plan.expect(7.0 + 2.7 * n, "a", functools.partial(proj_w.a_pass, n))
         for chunk in range(2):
-            plan.expect(9.0 + 1.9 * (2 * n - 1 + chunk), "b", functools.partial(proj_w.b_step, n, chunk))
-    plan.expect(9.8, "z", summed_z)
-    plan.expect(11.5, "core", summed_core)
-    plan.expect(11.8, "collect", qkv_w.collect)
-    plan.expect(14.5, "y", over_y.wait)
+            plan.expect(8.8 + 1.8 * (2 * n - 1 + chunk), "b", functools.partial(proj_w.b_step, n, chunk))
+    plan.expect(7.1 + 2.7 * steps, "a", proj_w.a_near)
+    plan.expect(10.0 + 2.7 * steps, "a far", proj_w.a_far)
+    plan.expect(8.8, "z", summed_z)
+    plan.expect(10.5, "core", summed_core)
+    plan.expect(10.6, "collect", qkv_w.collect)
+    plan.expect(13.0, "y", over_y.wait)
     for h in range(pairs):
         for frame in range(frames):
-            plan.expect(13.5 + 5.8 * h + 0.1 * frame, f"halo{h}", halo_copy(frame, h).wait_recv)
-    plan.expect(19.2, "up", qkv_w.up)
-    qkv_done = 14.5
+            plan.expect(11.8 + 5.8 * h + 0.1 * frame, f"halo{h}", halo_copy(frame, h).wait_recv)
+    plan.expect(6.1 + 5.8 * pairs, "up", qkv_w.up)
+    qkv_done = 12.6
     for step, way, chunk in qkv_w.first.each():
-        time = (13.5 if way else 20.0) + 1.8 * (2 * step - 1 + chunk)
+        time = (12.6 if way else 8.1 + 5.8 * pairs) + 1.7 * (2 * step - 1 + chunk)
         qkv_done = max(qkv_done, time)
         plan.expect(time, "qkv", functools.partial(qkv_w.first.step, step, way, chunk))
     plan.expect(qkv_done + 0.1, "rest", qkv_w.rest)
-    plan.expect(qkv_done + 1.0, "qkv", functools.partial(qkv_w.wait, 0))
+    plan.expect(qkv_done + 3.6, "qkv", functools.partial(qkv_w.wait, 0))
     for step, way, chunk in qkv_w.last.each():
-        plan.expect(qkv_done + 4.0 + 2.5 * step, "qkv last", functools.partial(qkv_w.last.step, step, way, chunk))
-    plan.expect(qkv_done + 6.0 + 2.5 * max(qkv_w.last.reach), "qkv last", functools.partial(qkv_w.wait, 1))
+        plan.expect(qkv_done + 5.0 + 2.5 * step, "qkv last", functools.partial(qkv_w.last.step, step, way, chunk))
+    plan.expect(qkv_done + 7.0 + 2.5 * max(qkv_w.last.reach), "qkv last", functools.partial(qkv_w.wait, 1))
 
     def split_taps():
         weight_loads[0].wait()
@@ -591,6 +591,12 @@
         plan.run(0.7, lambda: [activate(feat, frame, h, 2 + frame) for h in range(pairs)])
     plan.run(0.5, lambda: convolve(0, every, [(2, 0)], True))
     plan.run(1.0, lambda: convolve(1, every, [(3, 0), (2, 1)], True))
+    def split_quarter(half, part):
+        at = 2 * half + part
+        high, low = split(proj_all[half, part].reshape(width, wide))
+        proj_hi[at] = high
+        proj_lo[at] = low
+
     for h in range(pairs):
         for frame in range(frames):
             plan.run(0.35, lambda: activate(halo, frame, h, frame), f"halo{h}")
@@ -619,34 +625,42 @@
 
     def quarter_of(half, part):
         at = 2 * half + part
-        return dot3((band_hi[at], band_lo[at]), split(proj_all[half, part].reshape(width, wide)), NT)
-
-    made = plan.run(0.7, lambda: quarter_of(k.core, 0), "a far")
-    made = made + plan.run(0.7, lambda: quarter_of(k.core, 1), "b")
+        return dot3((band_hi[at], band_lo[at]), (proj_hi[at], proj_lo[at]), NT)
+
+    other = 1 - k.core
+    plan.run(0.3, lambda: split_quarter(k.core, 0), "a far")
+    made = plan.run(0.5, lambda: quarter_of(k.core, 0))
     proj_w.wait(0)
-    made = made + plan.run(0.7, lambda: quarter_of(1 - k.core, 0))
+    plan.run(0.3, lambda: split_quarter(other, 0))
+    made = made + plan.run(0.5, lambda: quarter_of(other, 0))
+    plan.run(0.3, lambda: split_quarter(k.core, 1), "b")
+    made = made + plan.run(0.5, lambda: quarter_of(k.core, 1))
     proj_w.wait(1)
-    made = made + plan.run(0.7, lambda: quarter_of(1 - k.core, 1))
+    plan.run(0.3, lambda: split_quarter(other, 1))
+    made = made + plan.run(0.5, lambda: quarter_of(other, 1))
     tokens[...] = made
     keys[z] = made
     queries[x] = made
 
     part_rows = count // 2
-    key_ring = Ring(z, z_count, k.z_device, lambda at, c: keys.at[at, pl.ds(c * part_rows, part_rows)],
-                    key_s, key_r, (steps, steps), 2)
+    key_chunks = 4
+    key_rows = count // key_chunks
+    key_ring = Ring(z, z_count, k.z_device, lambda at, c: keys.at[at, pl.ds(c * key_rows, key_rows)],
+                    key_s, key_r, (steps, steps), key_chunks)
     query_ring = Ring(x, X, k.x_device, lambda at, c: queries.at[at], query_s, query_r, (X // 2, X // 2), 1,
                       lambda ref, way: ref.at[pl.ds(way * part_rows, part_rows)])
     for way in BOTH:
         query_ring.start(way, 0)
-    for chunk in range(2):
+    for chunk in range(key_chunks):
         for way in BOTH:
             key_ring.start(way, chunk)
     begin = plan.now
     for step, way, chunk in key_ring.each():
-        plan.expect(begin + 1.5 + 2.9 * (2 * step - 1 + chunk) - (2.9 * chunk if step == steps else 0.0), f"key{step}",
+        turn = chunk if step < steps else chunk % (key_chunks // 2)
+        plan.expect(begin + 2.0 + 1.5 * (key_chunks * (step - 1) + turn + 1), f"key{step}",
                     functools.partial(key_ring.step, step, way, chunk))
     for step, way, chunk in query_ring.each():
-        plan.expect(begin + 4.4 * step + 3.0, "queries", functools.partial(query_ring.step, step, way, chunk))
+        plan.expect(begin + 4.9 * step + 2.9, "queries", functools.partial(query_ring.step, step, way, chunk))
 
     token_group = width // GROUPS
     sums = jnp.concatenate(
@@ -708,29 +722,31 @@
     def key_block(at):
         return normed(jnp.concatenate([keys[mod(z + away, z_count)] for away in sets[at]], axis=0))
 
-    def attend(step, at, block):
-        rows_of = lambda ref: ref[at].reshape(-1, ref.shape[-1])
-        scores = dot3((rows_of(q_hi), rows_of(q_lo)), block, NT)
+    def rows_of(ref, at):
+        return ref[at].reshape(-1, ref.shape[-1])
+
+    def scores_of(at, block):
+        return dot3((rows_of(q_hi, at), rows_of(q_lo, at)), block, NT)
+
+    def attend(first, at, block, scores):
         here = jnp.max(scores, axis=1, keepdims=True)
-        if step == 0:
-            new_top = here
-            weights = jnp.exp(scores - new_top)
-            new_mass = jnp.sum(weights, axis=1, keepdims=True)
-            value = dot3(split(weights), block)
-        else:
-            new_top = jnp.maximum(rows_of(top), here)
-            fade = jnp.exp(rows_of(top) - new_top)
-            weights = jnp.exp(scores - new_top)
-            new_mass = rows_of(mass) * fade + jnp.sum(weights, axis=1, keepdims=True)
-            value = rows_of(total) * fade + dot3(split(weights), block)
-        return new_top, new_mass, value
-
-    def attend_all(step):
-        for ref, value in zip((top, mass, total), attend(step, slice(None), key_block(step))):
+        if first:
+            weights = jnp.exp(scores - here)
+            return here, jnp.sum(weights, axis=1, keepdims=True), dot3(split(weights), block)
+        new_top = jnp.maximum(rows_of(top, at), here)
+        fade = jnp.exp(rows_of(top, at) - new_top)
+        weights = jnp.exp(scores - new_top)
+        new_mass = rows_of(mass, at) * fade + jnp.sum(weights, axis=1, keepdims=True)
+        return new_top, new_mass, rows_of(total, at) * fade + dot3(split(weights), block)
+
+    def attend_all(step, block, scores):
+        for ref, value in zip((top, mass, total), attend(step == 0, slice(None), block, scores)):
             ref[...] = value.reshape(ref.shape)
 
     for step in range(len(sets) - 1):
-        plan.run(3.0 if step == 0 else 2.2, lambda: attend_all(step), f"key{step + 1}")
+        block = plan.run(0.2, lambda: key_block(step), f"key{step + 1}")
+        scores = plan.run(1.2 if step == 0 else 0.9, lambda: scores_of(slice(None), block))
+        plan.run(1.6 if step == 0 else 1.2, lambda: attend_all(step, block, scores))
 
     half_rows = [pl.ds(way * part_rows, part_rows) for way in BOTH]
     toward = (1, -1)
@@ -759,7 +775,8 @@
     block = key_block(-1)
     for by in (2, 1, 3, 0):
         at = mod(x + by, X)
-        last_top, last_mass, value = attend(steps, pl.ds(at, 1), block)
+        this = pl.ds(at, 1)
+        last_top, last_mass, value = attend(False, this, block, scores_of(this, block))
         partial[at] = value / last_mass
         lse_mine[at] = jnp.transpose(jnp.broadcast_to(last_top + jnp.log(last_mass), (count, 128)))[0:1]
         if by == 2:
@@ -848,6 +865,7 @@
         vmem((4, half_h, 4 * half_w, channels), bf16), vmem((4, half_h, 4 * half_w, channels), bf16),
         vmem((frames, half_h, 4 * half_w, channels), f32),
         vmem((4, count, wide), bf16), vmem((4, count, wide), bf16),
+        vmem((4, width, wide), bf16), vmem((4, width, wide), bf16),
         vmem((count, width), f32),
         vmem((z_count, count, width), f32),
         vmem((X, count, width), f32),
@@ -859,7 +877,7 @@
         vmem((2, count, width), f32), vmem((2, 1, 128), f32),
         dma((6,)), dma((frames, half_h)), dma((frames, half_h)), dma((6,)), dma((6,)),
         *proj_sems, *qkv_sems,
-        dma((4, steps)), dma((4, steps)), dma((2, X // 2)), dma((2, X // 2)), dma((5, 2)), dma((5, 2)),
+        dma((8, steps)), dma((8, steps)), dma((2, X // 2)), dma((2, X // 2)), dma((5, 2)), dma((5, 2)),
     ]
     whole = pl.BlockSpec(memory_space=vmem)
     anywhere = pl.BlockSpec(memory_space=pl.ANY)

time: 90.6 us -> 86.6 us (0.956)
  Pallas kernels: 88.7 us -> 84.7 us
    pallas_call x1, Pallas kernels: 88.7 us -> 84.7 us  [shards(): pl.pallas_call(functools.partial(kernel, z_count, tm_count), out_shape=ja...]
where the time goes in v3:
time: 86.6 us; the launch traced here: 86.4 us
  Pallas kernels  84.7 us (98%)
  local copies, waits for them, and re-layouts  1.67 us (2%)
    pallas_call x1, Pallas kernels, shards(): pl.pallas_call(functools.partial(kernel, z_count, tm_count), out_shape=ja...  84.7 us

profile of v3, /device:TPU:6, one launch (start us, length us, event | category | flops | bytes accessed | tf_op | source)
XLA Modules:
  0.0 86.4 jit_solution(11913729246098447672)
XLA Ops:
  0.0 84.7 %shard_map.73 = f32[1,2,64,512]{3,2,1,0:T(8,128)} custom-call(f32[2,4,128,256]{3,2,1,0:T(8,128)} %features.1, f32[1,256]{1,0:T(1,128)} %bitcast.7, f32[3,256,256]{2,1,0:T(8,128)} %conv.1, f32[16,2048]{1,0:T(8,128)} %bitcast.4, f32[1,512]{1,0:T(1,128)} %bitcast.6, f32[48,512]{1,0:T(8,128)} %bitcast.5, f32[512,512]{1,0:T(8,128)} %out_weight.1), custom_call_target="tpu_custom_call" | custom-call | tf_op jit(solution)/shard_map/pallas_call | solution.py:884
  84.7 1.7 %copy.9 = f32[1,2,64,512]{3,2,1,0:T(8,128)} copy(f32[1,2,64,512]{3,2,1,0:T(8,128)} %shard_map.73) | data formatting | bytes 524288

commit v4 on v3

--- a/solution.py
+++ b/solution.py
@@ -11,7 +11,6 @@
 GROUPS = 32
 X = 4
 epsilon = 1e-06
-highest = lax.Precision.HIGHEST
 f32, bf16 = jnp.float32, jnp.bfloat16
 NN = (((1,), (0,)), ((), ()))
 NT = (((1,), (1,)), ((), ()))
@@ -36,8 +35,21 @@
     return by_high[:rows] + (by_high[rows:] + dot(a[0], b[1], dims))
 
 
-def exact(a, b):
-    return lax.dot_general(a, b, NN, precision=highest, preferred_element_type=f32)
+def dot3_turned(a, b):
+    rows = a[0].shape[0]
+    by_high = dot(b[0], jnp.concatenate(a, axis=0), NT)
+    return by_high[:, :rows] + (by_high[:, rows:] + dot(b[1], a[0], NT))
+
+
+def exact(a, table):
+    high = a.astype(bf16)
+    rest = a - high.astype(f32)
+    middle = rest.astype(bf16)
+    low = (rest - middle.astype(f32)).astype(bf16)
+    rows = a.shape[0]
+    parts = jnp.concatenate([part.astype(f32) for part in (high, middle, low)] + [jnp.zeros_like(a)], axis=0).astype(bf16)
+    by_part = dot(parts, table.astype(bf16), NN)
+    return by_part[:rows] + (by_part[rows : 2 * rows] + by_part[2 * rows : 3 * rows])
 
 
 def iota(shape, axis):
@@ -625,7 +637,7 @@
 
     def quarter_of(half, part):
         at = 2 * half + part
-        return dot3((band_hi[at], band_lo[at]), (proj_hi[at], proj_lo[at]), NT)
+        return dot3_turned((band_hi[at], band_lo[at]), (proj_hi[at], proj_lo[at]))
 
     other = 1 - k.core
     plan.run(0.3, lambda: split_quarter(k.core, 0), "a far")
@@ -638,6 +650,7 @@
     proj_w.wait(1)
     plan.run(0.3, lambda: split_quarter(other, 1))
     made = made + plan.run(0.5, lambda: quarter_of(other, 1))
+    made = jnp.transpose(made)
     tokens[...] = made
     keys[z] = made
     queries[x] = made
@@ -710,8 +723,11 @@
         query_weight = tuple(jnp.transpose(part.astype(f32)).astype(bf16) for part in columns_of(0))
         return split(dot3(query_weight, columns_of(1)) * (1.0 / math.sqrt(float(width))))
 
+    order = (2, 1, 3, 0)
+
     def ask():
-        high, low = split(dot3(normed(queries[...].reshape(X * count, width)), query_key))
+        asking = jnp.concatenate([queries[mod(x + by, X)] for by in order], axis=0)
+        high, low = split(dot3(normed(asking), query_key))
         q_hi[...], q_lo[...] = high.reshape(q_hi.shape), low.reshape(q_lo.shape)
 
     query_key = plan.run(2.0, query_key_weight, "qkv")
@@ -755,12 +771,11 @@
         return copy(src, dst, part_s.at[kind, way], part_r.at[kind, way], k.x_device(toward[way]))
 
     def opposite(way):
-        at = mod(x + 2, X)
-        return (send(0, way, partial.at[at, half_rows[way]], relay.at[way]),
-                send(1, way, lse_mine.at[at], relay_lse.at[way]))
+        return (send(0, way, partial.at[0, half_rows[way]], relay.at[way]),
+                send(1, way, lse_mine.at[0], relay_lse.at[way]))
 
     def plain(way):
-        return (send(2, way, partial.at[mod(x + toward[way], X), half_rows[1 - way]], parts.at[way, half_rows[1 - way]]),)
+        return (send(2, way, partial.at[1 + way, half_rows[1 - way]], parts.at[way, half_rows[1 - way]]),)
 
     def joined(way):
         return (send(3, way, joint.at[way], parts.at[way, half_rows[way]]), send(4, way, joint_lse.at[way], parts_lse.at[way]))
@@ -773,24 +788,22 @@
 
     plan.need(f"key{steps}")
     block = key_block(-1)
-    for by in (2, 1, 3, 0):
-        at = mod(x + by, X)
-        this = pl.ds(at, 1)
-        last_top, last_mass, value = attend(False, this, block, scores_of(this, block))
-        partial[at] = value / last_mass
-        lse_mine[at] = jnp.transpose(jnp.broadcast_to(last_top + jnp.log(last_mass), (count, 128)))[0:1]
-        if by == 2:
-            for one in (*opposite(0), *opposite(1)):
+    for first, last in ((0, 1), (1, X)):
+        at = slice(first, last)
+        last_top, last_mass, value = attend(False, at, block, scores_of(at, block))
+        partial[at] = (value / last_mass).reshape(last - first, count, width)
+        lse = last_top + jnp.log(last_mass)
+        for i in range(first, last):
+            column = lse[(i - first) * count : (i + 1 - first) * count]
+            lse_mine[i] = jnp.transpose(jnp.broadcast_to(column, (count, 128)))[0:1]
+        for way in BOTH:
+            for one in opposite(way) if first == 0 else plain(way):
                 one.start()
-        elif by:
-            plain(0 if by == 1 else 1)[0].start()
     plan.now += 1.5
 
     def value_to_out():
         weight_loads[1].wait()
-        value_weight = columns_of(2)
-        value_weight = tuple(jnp.transpose(part.astype(f32)).astype(bf16) for part in value_weight)
-        return split(dot3(value_weight, split(out_in[...])))
+        return split(dot3(split(jnp.transpose(out_in[...])), columns_of(2)))
 
     value_out = plan.run(2.0, value_to_out, "qkv last")
     plan.upto(1e9)
@@ -798,7 +811,7 @@
     for way in BOTH:
         for one in opposite(way):
             one.wait_recv()
-        at = mod(x + toward[way], X)
+        at = 1 + way
         own, theirs = lse_mine[at], relay_lse[way]
         both = jnp.maximum(own, theirs)
         both = both + jnp.log(jnp.exp(own - both) + jnp.exp(theirs - both))
@@ -823,14 +836,14 @@
     for way in BOTH:
         for one in (*plain(way), *joined(way)):
             one.wait_recv()
-    given = [(lse_mine[x], partial[x])] + [(parts_lse[way], parts[way]) for way in BOTH]
+    given = [(lse_mine[3], partial[3])] + [(parts_lse[way], parts[way]) for way in BOTH]
     highest_lse = functools.reduce(jnp.maximum, [lse for lse, _ in given])
     shares = [jnp.exp(lse - highest_lse) for lse, _ in given]
     whole = functools.reduce(jnp.add, shares)
     merged = jnp.zeros((count, width), f32)
     for share, (_, value) in zip(shares, given):
         merged = merged + value * across(as_column(share / whole))
-    encoded = tokens[...] + dot3(split(merged), value_out)
+    encoded = tokens[...] + jnp.transpose(dot3_turned(split(merged), value_out))
     out[...] = encoded.reshape(out.shape)
 
     for way in BOTH:

time: 86.6 us -> 87.7 us (1.013)
  Pallas kernels: 84.7 us -> 85.6 us
where the time goes in v4:
time: 87.7 us; the launch traced here: 87.3 us
  Pallas kernels  85.6 us (98%)
  local copies, waits for them, and re-layouts  1.67 us (2%)
    pallas_call x1, Pallas kernels, shards(): pl.pallas_call(functools.partial(kernel, z_count, tm_count), out_shape=ja...  85.6 us

profile of v4, /device:TPU:6, one launch (start us, length us, event | category | flops | bytes accessed | tf_op | source)
XLA Modules:
  0.0 87.3 jit_solution(10427559178610147782)
XLA Ops:
  0.0 85.6 %shard_map.73 = f32[1,2,64,512]{3,2,1,0:T(8,128)} custom-call(f32[2,4,128,256]{3,2,1,0:T(8,128)} %features.1, f32[1,256]{1,0:T(1,128)} %bitcast.7, f32[3,256,256]{2,1,0:T(8,128)} %conv.1, f32[16,2048]{1,0:T(8,128)} %bitcast.4, f32[1,512]{1,0:T(1,128)} %bitcast.6, f32[48,512]{1,0:T(8,128)} %bitcast.5, f32[512,512]{1,0:T(8,128)} %out_weight.1), custom_call_target="tpu_custom_call" | custom-call | tf_op jit(solution)/shard_map/pallas_call | solution.py:897
  85.6 1.7 %copy.9 = f32[1,2,64,512]{3,2,1,0:T(8,128)} copy(f32[1,2,64,512]{3,2,1,0:T(8,128)} %shard_map.73) | data formatting | bytes 524288

commit v5 on v4

--- a/solution.py
+++ b/solution.py
@@ -33,12 +33,6 @@
         return dot(jnp.concatenate((a[0], a[1], a[0]), axis=1), jnp.concatenate(deep, axis=dims[0][1][0]), dims)
     by_high = dot(jnp.concatenate(a, axis=0), b[0], dims)
     return by_high[:rows] + (by_high[rows:] + dot(a[0], b[1], dims))
-
-
-def dot3_turned(a, b):
-    rows = a[0].shape[0]
-    by_high = dot(b[0], jnp.concatenate(a, axis=0), NT)
-    return by_high[:, :rows] + (by_high[:, rows:] + dot(b[1], a[0], NT))
 
 
 def exact(a, table):
@@ -110,6 +104,9 @@
 
     def y_device(self, by):
         return {"tm": mod(self.y + by, self.y_count) * 2 + self.core}
+
+    def tm_device(self, by):
+        return {"tm": mod(self.tm + by, 2 * self.y_count)}
 
     def sibling(self):
         return {"tm": self.tm + 1 - 2 * self.core}
@@ -423,7 +420,7 @@
     barrier = pltpu.get_barrier_semaphore()
     peers = (
         [k.x_device(by) for by in range(1, X)] + [k.z_device(by) for by in range(1, z_count)]
-        + [k.y_device(by) for by in range(1, k.y_count)] + [k.sibling(), {"tm": mod(tm - 1 + 2 * k.core, tm_count)}]
+        + [k.tm_device(by) for by in range(1, tm_count)]
     )
     for peer in peers:
         pl.semaphore_signal(barrier, inc=1, device_id=peer, device_id_type=pl.DeviceIdType.MESH)
@@ -465,24 +462,21 @@
     def lanes_of(rows_of_sums, table):
         return jnp.sum(jnp.where(lane // GROUPS == row, exact(rows_of_sums, table), 0.0), axis=0, keepdims=True)
 
-    x_sums[x] = lanes_of(stacked, fold)
+    slab_sums[tm] = lanes_of(stacked, fold)
     for one in quarters:
         one.wait()
 
     def exchange(slots, index, per, size, device, n):
         return Sums(slots, index, per, size, device, sum_s.at[n], sum_r.at[n])
 
-    over_x = exchange(x_sums, x, 1, X, k.x_device, 0)
-    over_z = exchange(z_sums, z, 1, z_count, k.z_device, 1)
-    over_y = exchange(slab_sums, k.y, 2, k.y_count, k.y_device, 2)
-    tokens_x = exchange(token_x, x, 1, X, k.x_device, 3)
-    tokens_z = exchange(token_z, z, 1, z_count, k.z_device, 4)
-
-    def slab_copy(at):
-        return copy(slab_sums.at[at], slab_sums.at[at], sum_s.at[5], sum_r.at[5], k.sibling())
+    over_tm = exchange(slab_sums, tm, 1, tm_count, k.tm_device, 0)
+    over_x = exchange(x_sums, x, 1, X, k.x_device, 1)
+    over_z = exchange(z_sums, z, 1, z_count, k.z_device, 2)
+    tokens_z = exchange(token_z, z, 1, z_count, k.z_device, 3)
+    tokens_x = exchange(token_x, x, 1, X, k.x_device, 4)
 
     pl.semaphore_wait(barrier, len(peers))
-    over_x.start()
+    over_tm.start()
     pairs = height // 2
 
     def halo_copy(f, h):
@@ -496,21 +490,18 @@
     qkv_w.start()
     plan.now = 4.0
 
+    def summed_tm():
+        over_tm.wait()
+        x_sums[x] = jnp.concatenate([slab_sums[i] for i in range(tm_count)], axis=0)
+        over_x.start()
+
     def summed_x():
         over_x.wait()
         z_sums[z] = jnp.sum(x_sums[...], axis=0)
         over_z.start()
 
-    def summed_z():
-        over_z.wait()
-        slab_sums[tm] = jnp.sum(z_sums[...], axis=0)
-        slab_copy(tm).start()
-
-    def summed_core():
-        slab_copy(tm + 1 - 2 * k.core).wait_recv()
-        over_y.start()
-
-    plan.expect(6.3, "x", summed_x)
+    plan.expect(6.4, "tm", summed_tm)
+    plan.expect(9.0, "x", summed_x)
     plan.expect(7.8, "qkv x", qkv_w.across)
     plan.expect(6.8, "b", proj_w.b_start)
     plan.expect(7.5, "a", functools.partial(proj_w.a_pass, 0))
@@ -521,10 +512,8 @@
             plan.expect(8.8 + 1.8 * (2 * n - 1 + chunk), "b", functools.partial(proj_w.b_step, n, chunk))
     plan.expect(7.1 + 2.7 * steps, "a", proj_w.a_near)
     plan.expect(10.0 + 2.7 * steps, "a far", proj_w.a_far)
-    plan.expect(8.8, "z", summed_z)
-    plan.expect(10.5, "core", summed_core)
     plan.expect(10.6, "collect", qkv_w.collect)
-    plan.expect(13.0, "y", over_y.wait)
+    plan.expect(12.0, "z", over_z.wait)
     for h in range(pairs):
         for frame in range(frames):
             plan.expect(11.8 + 5.8 * h + 0.1 * frame, f"halo{h}", halo_copy(frame, h).wait_recv)
@@ -547,11 +536,13 @@
     taps = plan.run(0.4, split_taps)
 
     def statistics():
-        everything = slab_sums[...]
+        everything = jnp.sum(z_sums[...], axis=0)
         slab = iota(everything.shape, 0)
-        earlier = jnp.sum(jnp.where(slab < tm - 1, everything, 0.0), axis=0)
-        previous = jnp.sum(jnp.where(slab == tm - 1, everything, 0.0), axis=0)
-        own = jnp.sum(jnp.where(slab == tm, everything, 0.0), axis=0)
+
+        def of(these):
+            return jnp.sum(jnp.where(these, everything, 0.0), axis=0, keepdims=True)
+
+        earlier, previous, own = of(slab < tm - 1), of(slab == tm - 1), of(slab == tm)
         kind, upto = row % 2, row // 2
         lane_kind, lane_frame = lane // GROUPS % 2, lane // GROUPS // 2
         mine = lane_kind == kind
@@ -572,7 +563,7 @@
             scales.append(rsqrt(variance))
         return means, scales
 
-    means, scales = plan.run(0.6, statistics, "y")
+    means, scales = plan.run(0.6, statistics, "z")
     norm_gain = gain[...]
 
     def cells_of(src, frame, h, b, c):
@@ -637,7 +628,7 @@
 
     def quarter_of(half, part):
         at = 2 * half + part
-        return dot3_turned((band_hi[at], band_lo[at]), (proj_hi[at], proj_lo[at]))
+        return dot3((band_hi[at], band_lo[at]), (proj_hi[at], proj_lo[at]), NT)
 
     other = 1 - k.core
     plan.run(0.3, lambda: split_quarter(k.core, 0), "a far")
@@ -650,7 +641,6 @@
     proj_w.wait(1)
     plan.run(0.3, lambda: split_quarter(other, 1))
     made = made + plan.run(0.5, lambda: quarter_of(other, 1))
-    made = jnp.transpose(made)
     tokens[...] = made
     keys[z] = made
     queries[x] = made
@@ -662,8 +652,14 @@
                     key_s, key_r, (steps, steps), key_chunks)
     query_ring = Ring(x, X, k.x_device, lambda at, c: queries.at[at], query_s, query_r, (X // 2, X // 2), 1,
                       lambda ref, way: ref.at[pl.ds(way * part_rows, part_rows)])
-    for way in BOTH:
-        query_ring.start(way, 0)
+    token_group = width // GROUPS
+    sums = jnp.concatenate(
+        [jnp.sum(made, axis=0, keepdims=True), jnp.sum(made * made, axis=0, keepdims=True), jnp.zeros((6, width), f32)],
+        axis=0,
+    )
+    fold = (iota((width, 128), 1) % GROUPS == iota((width, 128), 0) // token_group).astype(f32)
+    token_z[z] = lanes_of(sums, fold)
+    tokens_z.start()
     for chunk in range(key_chunks):
         for way in BOTH:
             key_ring.start(way, chunk)
@@ -672,35 +668,28 @@
         turn = chunk if step < steps else chunk % (key_chunks // 2)
         plan.expect(begin + 2.0 + 1.5 * (key_chunks * (step - 1) + turn + 1), f"key{step}",
                     functools.partial(key_ring.step, step, way, chunk))
+
+    def token_summed_z():
+        tokens_z.wait()
+        token_x[x] = jnp.sum(token_z[...], axis=0)
+        tokens_x.start()
+        for way in BOTH:
+            query_ring.start(way, 0)
+
+    plan.expect(begin + 2.5, "tokens z", token_summed_z)
+    plan.expect(begin + 5.0, "tokens x", tokens_x.wait)
     for step, way, chunk in query_ring.each():
-        plan.expect(begin + 4.9 * step + 2.9, "queries", functools.partial(query_ring.step, step, way, chunk))
-
-    token_group = width // GROUPS
-    sums = jnp.concatenate(
-        [jnp.sum(made, axis=0, keepdims=True), jnp.sum(made * made, axis=0, keepdims=True), jnp.zeros((6, width), f32)],
-        axis=0,
-    )
-    fold = (iota((width, 128), 1) % GROUPS == iota((width, 128), 0) // token_group).astype(f32)
-    token_x[x] = lanes_of(sums, fold)
-    tokens_x.start()
-
-    def token_summed_x():
-        tokens_x.wait()
-        token_z[z] = jnp.sum(token_x[...], axis=0)
-        tokens_z.start()
-
-    plan.expect(begin + 2.5, "tokens x", token_summed_x)
-    plan.expect(begin + 5.0, "tokens z", tokens_z.wait)
+        plan.expect(begin + 4.9 * step + 5.2, "queries", functools.partial(query_ring.step, step, way, chunk))
 
     def token_statistics():
-        all_sums = jnp.sum(token_z[...], axis=0)
+        all_sums = jnp.sum(token_x[...], axis=0)
         unfold = (iota((128, width), 0) % GROUPS == iota((128, width), 1) // token_group).astype(f32)
         spread_sums = exact(jnp.where(lane // GROUPS == row, all_sums, 0.0), unfold)
         token_count = float(rows_count * count * token_group)
         mean = spread_sums[0:1] / token_count
         return mean, rsqrt(spread_sums[1:2] / token_count - mean * mean)
 
-    token_mean, token_scale = plan.run(0.6, token_statistics, "tokens z")
+    token_mean, token_scale = plan.run(0.6, token_statistics, "tokens x")
     token_gain = attn_gain[...]
 
     def normed(value):
@@ -803,7 +792,8 @@
 
     def value_to_out():
         weight_loads[1].wait()
-        return split(dot3(split(jnp.transpose(out_in[...])), columns_of(2)))
+        value_weight = tuple(jnp.transpose(part.astype(f32)).astype(bf16) for part in columns_of(2))
+        return split(dot3(value_weight, split(out_in[...])))
 
     value_out = plan.run(2.0, value_to_out, "qkv last")
     plan.upto(1e9)
@@ -828,9 +818,8 @@
     qkv_w.finish()
     for one in halo_copies:
         one.wait_send()
-    for one in (over_x, over_z, over_y, tokens_x, tokens_z):
+    for one in (over_tm, over_x, over_z, tokens_x, tokens_z):
         one.finish()
-    slab_copy(tm).wait_send()
     key_ring.finish()
     query_ring.finish()
     for way in BOTH:
@@ -843,7 +832,7 @@
     merged = jnp.zeros((count, width), f32)
     for share, (_, value) in zip(shares, given):
         merged = merged + value * across(as_column(share / whole))
-    encoded = tokens[...] + jnp.transpose(dot3_turned(split(merged), value_out))
+    encoded = tokens[...] + dot3(split(merged), value_out)
     out[...] = encoded.reshape(out.shape)
 
     for way in BOTH:
@@ -871,7 +860,7 @@
     scratch = [
         vmem((2, frames, height, columns, 128), f32), vmem((2, frames, height, columns, 128), f32),
         vmem(conv_weight.shape, f32), vmem(out_weight.shape, f32),
-        vmem((X, 1, 128), f32), vmem((z_count, 1, 128), f32), vmem((tm_count, 1, 128), f32),
+        vmem((X, tm_count, 128), f32), vmem((z_count, tm_count, 128), f32), vmem((tm_count, 1, 128), f32),
         vmem((X, 1, 128), f32), vmem((z_count, 1, 128), f32),
         vmem((2, 2, z_count, X, proj_rows, wide), f32),
         vmem((2, y_count, z_count // 2, X, qkv_rows, narrow), f32),

time: 87.7 us -> 87.6 us (level)
  the two profiles are of different devices: /device:TPU:6 before, /device:TPU:22 now
where the time goes in v5:
time: 87.6 us; the launch traced here: 87.4 us
  Pallas kernels  85.7 us (98%)
  local copies, waits for them, and re-layouts  1.67 us (2%)
    pallas_call x1, Pallas kernels, shards(): pl.pallas_call(functools.partial(kernel, z_count, tm_count), out_shape=ja...  85.7 us

profile of v5, /device:TPU:22, one launch (start us, length us, event | category | flops | bytes accessed | tf_op | source)
XLA Modules:
  0.0 87.4 jit_solution(3341781321808921423)
XLA Ops:
  0.0 85.7 %shard_map.73 = f32[1,2,64,512]{3,2,1,0:T(8,128)} custom-call(f32[2,4,128,256]{3,2,1,0:T(8,128)} %features.1, f32[1,256]{1,0:T(1,128)} %bitcast.7, f32[3,256,256]{2,1,0:T(8,128)} %conv.1, f32[16,2048]{1,0:T(8,128)} %bitcast.4, f32[1,512]{1,0:T(1,128)} %bitcast.6, f32[48,512]{1,0:T(8,128)} %bitcast.5, f32[512,512]{1,0:T(8,128)} %out_weight.1), custom_call_target="tpu_custom_call" | custom-call | tf_op jit(solution)/shard_map/pallas_call | solution.py:886
  85.7 1.7 %copy.9 = f32[1,2,64,512]{3,2,1,0:T(8,128)} copy(f32[1,2,64,512]{3,2,1,0:T(8,128)} %shard_map.73) | data formatting | bytes 524288

commit v6 on v5

--- a/solution.py
+++ b/solution.py
@@ -391,9 +391,9 @@
 
 def kernel(
     z_count, tm_count,
-    features, gain, conv, proj, attn_gain, qkv, out_weight, out,
+    features, gain, conv, proj, attn_gain, qkv, out_weight, tokens_out, out,
     feat, halo, conv_in, out_in, x_sums, z_sums, slab_sums, token_x, token_z,
-    proj_all, qkv_all, act_hi, act_lo, residual, band_hi, band_lo, proj_hi, proj_lo, tokens, keys, queries, q_hi, q_lo, total, top, mass,
+    proj_all, qkv_all, act_hi, act_lo, residual, band_hi, band_lo, proj_hi, proj_lo, keys, queries, q_hi, q_lo, total, top, mass,
     partial, lse_mine, relay, relay_lse, joint, joint_lse, parts, parts_lse,
     load_s, halo_s, halo_r, sum_s, sum_r, *sems,
 ):
@@ -405,7 +405,7 @@
     frames, height, columns, channels = features.shape
     half_w = columns // 2
     count = (height // 2) * half_w
-    width = tokens.shape[1]
+    width = keys.shape[2]
     wide = proj_all.shape[5]
     per_half, narrow = qkv_all.shape[4:]
     steps = z_count // 2
@@ -516,11 +516,11 @@
     plan.expect(12.0, "z", over_z.wait)
     for h in range(pairs):
         for frame in range(frames):
-            plan.expect(11.8 + 5.8 * h + 0.1 * frame, f"halo{h}", halo_copy(frame, h).wait_recv)
-    plan.expect(6.1 + 5.8 * pairs, "up", qkv_w.up)
+            plan.expect(13.0 + 7.0 * h + 0.1 * frame, f"halo{h}", halo_copy(frame, h).wait_recv)
+    plan.expect(6.2 + 7.0 * pairs, "up", qkv_w.up)
     qkv_done = 12.6
     for step, way, chunk in qkv_w.first.each():
-        time = (12.6 if way else 8.1 + 5.8 * pairs) + 1.7 * (2 * step - 1 + chunk)
+        time = (12.6 if way else 8.2 + 7.0 * pairs) + 1.7 * (2 * step - 1 + chunk)
         qkv_done = max(qkv_done, time)
         plan.expect(time, "qkv", functools.partial(qkv_w.first.step, step, way, chunk))
     plan.expect(qkv_done + 0.1, "rest", qkv_w.rest)
@@ -641,7 +641,7 @@
     proj_w.wait(1)
     plan.run(0.3, lambda: split_quarter(other, 1))
     made = made + plan.run(0.5, lambda: quarter_of(other, 1))
-    tokens[...] = made
+    tokens_out[...] = made.reshape(tokens_out.shape)
     keys[z] = made
     queries[x] = made
 
@@ -660,6 +660,8 @@
     fold = (iota((width, 128), 1) % GROUPS == iota((width, 128), 0) // token_group).astype(f32)
     token_z[z] = lanes_of(sums, fold)
     tokens_z.start()
+    for way in BOTH:
+        query_ring.start(way, 0)
     for chunk in range(key_chunks):
         for way in BOTH:
             key_ring.start(way, chunk)
@@ -673,13 +675,11 @@
         tokens_z.wait()
         token_x[x] = jnp.sum(token_z[...], axis=0)
         tokens_x.start()
-        for way in BOTH:
-            query_ring.start(way, 0)
 
     plan.expect(begin + 2.5, "tokens z", token_summed_z)
-    plan.expect(begin + 5.0, "tokens x", tokens_x.wait)
+    plan.expect(begin + 9.5, "tokens x", tokens_x.wait)
     for step, way, chunk in query_ring.each():
-        plan.expect(begin + 4.9 * step + 5.2, "queries", functools.partial(query_ring.step, step, way, chunk))
+        plan.expect(begin + 4.9 * step + 2.9, "queries", functools.partial(query_ring.step, step, way, chunk))
 
     def token_statistics():
         all_sums = jnp.sum(token_x[...], axis=0)
@@ -689,7 +689,6 @@
         mean = spread_sums[0:1] / token_count
         return mean, rsqrt(spread_sums[1:2] / token_count - mean * mean)
 
-    token_mean, token_scale = plan.run(0.6, token_statistics, "tokens x")
     token_gain = attn_gain[...]
 
     def normed(value):
@@ -720,6 +719,7 @@
         q_hi[...], q_lo[...] = high.reshape(q_hi.shape), low.reshape(q_lo.shape)
 
     query_key = plan.run(2.0, query_key_weight, "qkv")
+    token_mean, token_scale = plan.run(0.6, token_statistics, "tokens x")
     plan.run(1.5, ask, "queries")
 
     sets = [(0, -1, 1)] + [(-step, step) for step in range(2, steps)] + [(steps,)]
@@ -832,8 +832,7 @@
     merged = jnp.zeros((count, width), f32)
     for share, (_, value) in zip(shares, given):
         merged = merged + value * across(as_column(share / whole))
-    encoded = tokens[...] + dot3(split(merged), value_out)
-    out[...] = encoded.reshape(out.shape)
+    out[...] = dot3(split(merged), value_out).reshape(out.shape)
 
     for way in BOTH:
         for one in (*opposite(way), *plain(way), *joined(way)):
@@ -868,7 +867,6 @@
         vmem((frames, half_h, 4 * half_w, channels), f32),
         vmem((4, count, wide), bf16), vmem((4, count, wide), bf16),
         vmem((4, width, wide), bf16), vmem((4, width, wide), bf16),
-        vmem((count, width), f32),
         vmem((z_count, count, width), f32),
         vmem((X, count, width), f32),
         vmem((X, count, width), bf16), vmem((X, count, width), bf16),
@@ -883,14 +881,16 @@
     ]
     whole = pl.BlockSpec(memory_space=vmem)
     anywhere = pl.BlockSpec(memory_space=pl.ANY)
-    return pl.pallas_call(
+    given = jax.ShapeDtypeStruct((frames // 2, half_h, half_w, width), f32)
+    tokens, attended = pl.pallas_call(
         functools.partial(kernel, z_count, tm_count),
-        out_shape=jax.ShapeDtypeStruct((frames // 2, half_h, half_w, width), f32),
+        out_shape=(given, given),
         in_specs=[anywhere, whole, anywhere, anywhere, whole, anywhere, anywhere],
-        out_specs=whole,
+        out_specs=(whole, whole),
         scratch_shapes=scratch,
         compiler_params=pltpu.CompilerParams(collective_id=0, has_side_effects=True, vmem_limit_bytes=56 * 2**20),
     )(features, norm_gain[None], conv_weight, proj_weight.T, attn_gain[None], qkv_weight.T, out_weight)
+    return tokens + attended
 
 
 def solution(mesh):

time: 87.6 us -> 85.7 us (0.978)
  the two profiles are of different devices: /device:TPU:22 before, /device:TPU:6 now
where the time goes in v6:
time: 85.7 us; the launch traced here: 85.2 us
  Pallas kernels  83.5 us (97%)
  other arithmetic  1.77 us (2%)
    pallas_call x1, Pallas kernels, shards(): pl.pallas_call(functools.partial(kernel, z_count, tm_count), out_shape=(g...  83.5 us
    add x1, other arithmetic, shards(): return tokens + attended  1.77 us

profile of v6, /device:TPU:6, one launch (start us, length us, event | category | flops | bytes accessed | tf_op | source)
XLA Modules:
  0.0 85.2 jit_solution(3602534227207845342)
XLA Ops:
  0.0 83.5 %shard_map.73 = (f32[1,2,64,512]{3,2,1,0:T(8,128)}, f32[1,2,64,512]{3,2,1,0:T(8,128)}) custom-call(f32[2,4,128,256]{3,2,1,0:T(8,128)} %features.1, f32[1,256]{1,0:T(1,128)} %bitcast.7, f32[3,256,256]{2,1,0:T(8,128)} %conv.1, f32[16,2048]{1,0:T(8,128)} %bitcast.4, f32[1,512]{1,0:T(1,128)} %bitcast.6, f32[48,512]{1,0:T(8,128)} %bitcast.5, f32[512,512]{1,0:T(8,128)} %out_weight.1), custom_call_target="tpu_custom_call" | custom-call | tf_op jit(solution)/shard_map/pallas_call | solution.py:885
  83.5 1.8 %add.3 = f32[1,2,64,512]{3,2,1,0:T(8,128)} add(f32[1,2,64,512]{3,2,1,0:T(8,128)} %get-tuple-element.7, f32[1,2,64,512]{3,2,1,0:T(8,128)} %get-tuple-element.8) | non-fusion elementwise | flops 65536 | bytes 786432 | tf_op jit(solution)/shard_map/add | solution.py:893

commit v7 on v6

--- a/solution.py
+++ b/solution.py
@@ -477,13 +477,14 @@
 
     pl.semaphore_wait(barrier, len(peers))
     over_tm.start()
-    pairs = height // 2
-
-    def halo_copy(f, h):
-        at = (slice(None), f, pl.ds(2 * h, 2))
-        return copy(feat.at[at], halo.at[at], halo_s.at[f, h], halo_r.at[f, h], {"tm": mod(tm + 1, tm_count)})
-
-    halo_copies = [halo_copy(f, h) for h in range(pairs) for f in range(frames)]
+    groups = 2 * (height // 2)
+    group = count // groups
+
+    def halo_copy(f, g):
+        at = (slice(None), f, pl.ds(2 * (g // 2), 2), pl.ds(g % 2 * 2 * group, 2 * group))
+        return copy(feat.at[at], halo.at[at], halo_s.at[f, g], halo_r.at[f, g], {"tm": mod(tm + 1, tm_count)})
+
+    halo_copies = [halo_copy(f, g) for g in range(groups) for f in range(frames)]
     for one in halo_copies:
         one.start()
     proj_w.start()
@@ -514,13 +515,13 @@
     plan.expect(10.0 + 2.7 * steps, "a far", proj_w.a_far)
     plan.expect(10.6, "collect", qkv_w.collect)
     plan.expect(12.0, "z", over_z.wait)
-    for h in range(pairs):
+    for g in range(groups):
         for frame in range(frames):
-            plan.expect(13.0 + 7.0 * h + 0.1 * frame, f"halo{h}", halo_copy(frame, h).wait_recv)
-    plan.expect(6.2 + 7.0 * pairs, "up", qkv_w.up)
+            plan.expect(10.0 + 3.65 * g + 0.05 * frame, f"halo{g}", halo_copy(frame, g).wait_recv)
+    plan.expect(10.2 + 3.65 * (groups - 1), "up", qkv_w.up)
     qkv_done = 12.6
     for step, way, chunk in qkv_w.first.each():
-        time = (12.6 if way else 8.2 + 7.0 * pairs) + 1.7 * (2 * step - 1 + chunk)
+        time = (12.6 if way else 12.2 + 3.65 * (groups - 1)) + 1.7 * (2 * step - 1 + chunk)
         qkv_done = max(qkv_done, time)
         plan.expect(time, "qkv", functools.partial(qkv_w.first.step, step, way, chunk))
     plan.expect(qkv_done + 0.1, "rest", qkv_w.rest)
@@ -566,51 +567,33 @@
     means, scales = plan.run(0.6, statistics, "z")
     norm_gain = gain[...]
 
-    def cells_of(src, frame, h, b, c):
-        return jnp.concatenate([src[half, frame, 2 * h + b, pl.ds(c, half_w, stride=2), :] for half in range(2)], axis=1)
-
-    def activate(src, frame, h, at):
+    def cells_of(src, frame, g, b, c):
+        place = pl.ds(g % 2 * 2 * group + c, group, stride=2)
+        return jnp.concatenate([src[half, frame, 2 * (g // 2) + b, place, :] for half in range(2)], axis=1)
+
+    def activate(src, frame, g, at):
         for b in range(2):
             for c in range(2):
-                value = (cells_of(src, frame, h, b, c) - means[at]) * scales[at] * norm_gain
+                value = (cells_of(src, frame, g, b, c) - means[at]) * scales[at] * norm_gain
                 value = value / (1.0 + jnp.exp(-value))
                 if at < 2:
                     value = jnp.where(tm > 0, value, 0.0)
                 high, low = split(value)
-                place = pl.ds((2 * b + c) * half_w, half_w)
-                act_hi[at, h, place] = high
-                act_lo[at, h, place] = low
-
-    def activated(at, h):
-        return tuple(ref[at, h].reshape(-1, channels) for ref in (act_hi, act_lo))
-
-    def convolve(frame, h, terms, first=False):
-        value = functools.reduce(jnp.add, [dot3(activated(at, h), taps[lag]) for at, lag in terms])
-        value = value.reshape((-1, 4 * half_w, channels))
-        residual[frame, h] = value if first else residual[frame, h] + value
-
-    every = pl.ds(0, pairs)
-    for frame in range(frames):
-        plan.run(0.7, lambda: [activate(feat, frame, h, 2 + frame) for h in range(pairs)])
-    plan.run(0.5, lambda: convolve(0, every, [(2, 0)], True))
-    plan.run(1.0, lambda: convolve(1, every, [(3, 0), (2, 1)], True))
-    def split_quarter(half, part):
-        at = 2 * half + part
-        high, low = split(proj_all[half, part].reshape(width, wide))
-        proj_hi[at] = high
-        proj_lo[at] = low
-
-    for h in range(pairs):
-        for frame in range(frames):
-            plan.run(0.35, lambda: activate(halo, frame, h, frame), f"halo{h}")
-        plan.run(0.6, lambda: convolve(0, pl.ds(h, 1), [(1, 1), (0, 2)]))
-        plan.run(0.3, lambda: convolve(1, pl.ds(h, 1), [(1, 2)]))
-
-    def haar():
+                place = pl.ds((2 * b + c) * group, group)
+                act_hi[at, g, place] = high
+                act_lo[at, g, place] = low
+
+    def activated(at, these):
+        return tuple(ref[at, these].reshape(-1, channels) for ref in (act_hi, act_lo))
+
+    def convolve(frame, these, terms, first=False):
+        value = functools.reduce(jnp.add, [dot3(activated(at, these), taps[lag]) for at, lag in terms])
+        value = value.reshape((-1, 4 * group, channels))
+        residual[frame, these] = value if first else residual[frame, these] + value
+
+    def haar(g):
         bands = [
-            jnp.concatenate([
-                residual[a, h, pl.ds((2 * b + c) * half_w, half_w)] + cells_of(feat, a, h, b, c) for h in range(pairs)
-            ], axis=0)
+            residual[a, g, pl.ds((2 * b + c) * group, group)] + cells_of(feat, a, g, b, c)
             for a in range(2) for b in range(2) for c in range(2)
         ]
         for bit in (4, 2, 1):
@@ -619,19 +602,42 @@
             ]
         bands = [split(band * (1.0 / math.sqrt(8.0))) for band in bands]
         per_quarter = wide // channels
+        place = pl.ds(g * group, group)
         for quarter in range(4):
             ours = bands[quarter * per_quarter : (quarter + 1) * per_quarter]
-            band_hi[quarter] = jnp.concatenate([band[0] for band in ours], axis=1)
-            band_lo[quarter] = jnp.concatenate([band[1] for band in ours], axis=1)
-
-    plan.run(0.7, haar)
+            band_hi[quarter, place] = jnp.concatenate([band[0] for band in ours], axis=1)
+            band_lo[quarter, place] = jnp.concatenate([band[1] for band in ours], axis=1)
+
+    wide = proj_all.shape[5]
+
+    def split_quarter(half, part):
+        at = 2 * half + part
+        high, low = split(proj_all[half, part].reshape(width, wide))
+        proj_hi[at] = high
+        proj_lo[at] = low
 
     def quarter_of(half, part):
         at = 2 * half + part
         return dot3((band_hi[at], band_lo[at]), (proj_hi[at], proj_lo[at]), NT)
 
+    every = pl.ds(0, groups)
+    for frame in range(frames):
+        plan.run(0.7, lambda: [activate(feat, frame, g, 2 + frame) for g in range(groups)])
+    plan.run(0.5, lambda: convolve(0, every, [(2, 0)], True))
+    plan.run(1.0, lambda: convolve(1, every, [(3, 0), (2, 1)], True))
+
+    def join(g):
+        for frame in range(frames):
+            activate(halo, frame, g, frame)
+        convolve(0, pl.ds(g, 1), [(1, 1), (0, 2)])
+        convolve(1, pl.ds(g, 1), [(1, 2)])
+        haar(g)
+
     other = 1 - k.core
+    for g in range(groups - 1):
+        plan.run(1.2, lambda: join(g), f"halo{g}")
     plan.run(0.3, lambda: split_quarter(k.core, 0), "a far")
+    plan.run(1.2, lambda: join(groups - 1), f"halo{groups - 1}")
     made = plan.run(0.5, lambda: quarter_of(k.core, 0))
     proj_w.wait(0)
     plan.run(0.3, lambda: split_quarter(other, 0))
@@ -677,9 +683,9 @@
         tokens_x.start()
 
     plan.expect(begin + 2.5, "tokens z", token_summed_z)
-    plan.expect(begin + 9.5, "tokens x", tokens_x.wait)
+    plan.expect(begin + 7.7, "tokens x", tokens_x.wait)
     for step, way, chunk in query_ring.each():
-        plan.expect(begin + 4.9 * step + 2.9, "queries", functools.partial(query_ring.step, step, way, chunk))
+        plan.expect(begin + 4.9 * step + 2.9, ("near", "far")[step - 1], functools.partial(query_ring.step, step, way, chunk))
 
     def token_statistics():
         all_sums = jnp.sum(token_x[...], axis=0)
@@ -688,11 +694,6 @@
         token_count = float(rows_count * count * token_group)
         mean = spread_sums[0:1] / token_count
         return mean, rsqrt(spread_sums[1:2] / token_count - mean * mean)
-
-    token_gain = attn_gain[...]
-
-    def normed(value):
-        return split((value - token_mean) * token_scale * token_gain)
 
     def columns_of(block):
         lanes = []
@@ -713,14 +714,19 @@
 
     order = (2, 1, 3, 0)
 
-    def ask():
-        asking = jnp.concatenate([queries[mod(x + by, X)] for by in order], axis=0)
-        high, low = split(dot3(normed(asking), query_key))
-        q_hi[...], q_lo[...] = high.reshape(q_hi.shape), low.reshape(q_lo.shape)
+    def ask(first, last):
+        asking = jnp.concatenate([queries[mod(x + by, X)] for by in (2, 1, 3, 0)[first:last]], axis=0)
+        for ref, value in zip((q_hi, q_lo), split(dot3(normed(asking), query_key))):
+            ref[first:last] = value.reshape((last - first, count, width))
 
     query_key = plan.run(2.0, query_key_weight, "qkv")
     token_mean, token_scale = plan.run(0.6, token_statistics, "tokens x")
-    plan.run(1.5, ask, "queries")
+    token_gain = attn_gain[...]
+
+    def normed(value):
+        return split((value - token_mean) * token_scale * token_gain)
+
+    plan.run(1.3, lambda: ask(1, X), "near")
 
     sets = [(0, -1, 1)] + [(-step, step) for step in range(2, steps)] + [(steps,)]
 
@@ -744,14 +750,21 @@
         new_mass = rows_of(mass, at) * fade + jnp.sum(weights, axis=1, keepdims=True)
         return new_top, new_mass, rows_of(total, at) * fade + dot3(split(weights), block)
 
-    def attend_all(step, block, scores):
-        for ref, value in zip((top, mass, total), attend(step == 0, slice(None), block, scores)):
-            ref[...] = value.reshape(ref.shape)
-
-    for step in range(len(sets) - 1):
+    def attend_all(first, at, block, scores):
+        for ref, value in zip((top, mass, total), attend(first, at, block, scores)):
+            ref[at] = value.reshape(-1, count, value.shape[-1])
+
+    near, far, both = slice(1, X), slice(0, 1), slice(0, X)
+    block = plan.run(0.2, lambda: key_block(0), "key1")
+    scores = plan.run(1.0, lambda: scores_of(near, block))
+    plan.run(1.4, lambda: attend_all(True, near, block, scores))
+    plan.run(0.6, lambda: ask(0, 1), "far")
+    scores = plan.run(0.5, lambda: scores_of(far, block))
+    plan.run(0.6, lambda: attend_all(True, far, block, scores))
+    for step in range(1, len(sets) - 1):
         block = plan.run(0.2, lambda: key_block(step), f"key{step + 1}")
-        scores = plan.run(1.2 if step == 0 else 0.9, lambda: scores_of(slice(None), block))
-        plan.run(1.6 if step == 0 else 1.2, lambda: attend_all(step, block, scores))
+        scores = plan.run(0.9, lambda: scores_of(both, block))
+        plan.run(1.2, lambda: attend_all(False, both, block, scores))
 
     half_rows = [pl.ds(way * part_rows, part_rows) for way in BOTH]
     toward = (1, -1)
@@ -863,8 +876,8 @@
         vmem((X, 1, 128), f32), vmem((z_count, 1, 128), f32),
         vmem((2, 2, z_count, X, proj_rows, wide), f32),
         vmem((2, y_count, z_count // 2, X, qkv_rows, narrow), f32),
-        vmem((4, half_h, 4 * half_w, channels), bf16), vmem((4, half_h, 4 * half_w, channels), bf16),
-        vmem((frames, half_h, 4 * half_w, channels), f32),
+        vmem((4, 2 * half_h, 2 * half_w, channels), bf16), vmem((4, 2 * half_h, 2 * half_w, channels), bf16),
+        vmem((frames, 2 * half_h, 2 * half_w, channels), f32),
         vmem((4, count, wide), bf16), vmem((4, count, wide), bf16),
         vmem((4, width, wide), bf16), vmem((4, width, wide), bf16),
         vmem((z_count, count, width), f32),
@@ -875,7 +888,7 @@
         vmem((2, count // 2, width), f32), vmem((2, 1, 128), f32),
         vmem((2, count // 2, width), f32), vmem((2, 1, 128), f32),
         vmem((2, count, width), f32), vmem((2, 1, 128), f32),
-        dma((6,)), dma((frames, half_h)), dma((frames, half_h)), dma((6,)), dma((6,)),
+        dma((6,)), dma((frames, 2 * half_h)), dma((frames, 2 * half_h)), dma((6,)), dma((6,)),
         *proj_sems, *qkv_sems,
         dma((8, steps)), dma((8, steps)), dma((2, X // 2)), dma((2, X // 2)), dma((5, 2)), dma((5, 2)),
     ]

time: 85.7 us -> 86.2 us (level)
  no operation moved by 1% of the time
where the time goes in v7:
time: 86.2 us; the launch traced here: 86 us
  Pallas kernels  84.2 us (98%)
  other arithmetic  1.77 us (2%)
    pallas_call x1, Pallas kernels, shards(): pl.pallas_call(functools.partial(kernel, z_count, tm_count), out_shape=(g...  84.2 us
    add x1, other arithmetic, shards(): return tokens + attended  1.77 us

profile of v7, /device:TPU:6, one launch (start us, length us, event | category | flops | bytes accessed | tf_op | source)
XLA Modules:
  0.0 86.0 jit_solution(11257513834858532247)
XLA Ops:
  0.0 84.2 %shard_map.73 = (f32[1,2,64,512]{3,2,1,0:T(8,128)}, f32[1,2,64,512]{3,2,1,0:T(8,128)}) custom-call(f32[2,4,128,256]{3,2,1,0:T(8,128)} %features.1, f32[1,256]{1,0:T(1,128)} %bitcast.7, f32[3,256,256]{2,1,0:T(8,128)} %conv.1, f32[16,2048]{1,0:T(8,128)} %bitcast.4, f32[1,512]{1,0:T(1,128)} %bitcast.6, f32[48,512]{1,0:T(8,128)} %bitcast.5, f32[512,512]{1,0:T(8,128)} %out_weight.1), custom_call_target="tpu_custom_call" | custom-call | tf_op jit(solution)/shard_map/pallas_call | solution.py:898
  84.2 1.8 %add.3 = f32[1,2,64,512]{3,2,1,0:T(8,128)} add(f32[1,2,64,512]{3,2,1,0:T(8,128)} %get-tuple-element.7, f32[1,2,64,512]{3,2,1,0:T(8,128)} %get-tuple-element.8) | non-fusion elementwise | flops 65536 | bytes 786432 | tf_op jit(solution)/shard_map/add | solution.py:906

commit v8 on v7

--- a/solution.py
+++ b/solution.py
@@ -297,38 +297,33 @@
 class Qkv:
     def __init__(self, links, piece, buf, sems):
         self.k, self.buf, self.source = links, buf, piece
-        self.load_s, self.x_s, self.x_r, self.z_s, self.z_r, e_s, e_r, l_s, l_r, self.c_s, self.c_r = sems
+        self.load_s, x_s, x_r, self.z_s, self.z_r, e_s, e_r, l_s, l_r, self.c_s, self.c_r = sems
         self.zs, self.xs = buf.shape[2], buf.shape[3]
         self.early = early = self.zs * 3 // 4
-        up = (links.y_count - 1) // 3
-        reach = (up, links.y_count - 1 - up)
+        places, self.quarter = 4, lax.rem(links.y, 4)
+        reach = (1, 2)
         half = self.xs // 2
         mine = lambda y, *rest: buf.at[(links.core, y, *rest)]
-        self.first = Ring(links.y, links.y_count, links.y_device,
+        self.first = Ring(self.quarter, places, links.y_device,
                           lambda y, c: mine(y, pl.ds(0, early), pl.ds(c * half, half)),
                           e_s, e_r, reach, 2, None, lambda ref: self.hand(0, ref).start())
-        self.last = Ring(links.y, links.y_count, links.y_device, lambda y, c: mine(y, pl.ds(early, self.zs - early)),
+        self.last = Ring(self.quarter, places, links.y_device, lambda y, c: mine(y, pl.ds(early, self.zs - early)),
                          l_s, l_r, reach, 1, None, lambda ref: self.hand(1, ref).start())
+        halves = self.zs // 2
+        self.over_x = Ring(links.x, links.x_count, links.x_device, lambda x, c: mine(self.quarter, slice(None), x), x_s, x_r,
+                           (links.x_count // 2,) * 2, 1, lambda ref, way: ref.at[pl.ds(way * halves, halves)])
         self.sends = lax.rem(links.z, 2) == links.core
         self.zz = lax.div(links.z, 2)
 
     def load(self):
-        return pltpu.make_async_copy(self.source, self.buf.at[self.k.core, self.k.y, self.zz, self.k.x], self.load_s.at[0])
+        return pltpu.make_async_copy(self.source, self.buf.at[self.k.core, self.quarter, self.zz, self.k.x], self.load_s.at[0])
 
     def preload(self):
         pl.when(self.sends)(lambda: self.load().start())
 
     def z_copy(self, by):
-        ref = self.buf.at[self.k.core, self.k.y, self.zz, self.k.x]
-        return copy(ref, ref, self.z_s.at[0], self.z_r.at[0], self.k.z_device(by))
-
-    def x_copy(self, by):
-        ref = self.buf.at[self.k.core, self.k.y, :, self.k.x]
-        return copy(ref, ref, self.x_s.at[0], self.x_r.at[0], self.k.x_device(by))
-
-    def x_all(self):
-        ref = self.buf.at[self.k.core, self.k.y, :, pl.ds(0, self.xs - 1)]
-        return copy(ref, ref, self.x_s.at[0], self.x_r.at[0], self.k.x_device(1))
+        ref = self.buf.at[self.k.core, self.quarter, self.zz, self.k.x]
+        return copy(ref, ref, self.z_s.at[by], self.z_r.at[0], self.k.z_device(by))
 
     def start(self):
         @pl.when(self.sends)
@@ -339,20 +334,25 @@
 
     def across(self):
         def got(count):
-            ref = self.buf.at[self.k.core, self.k.y, pl.ds(0, count), self.k.x]
+            ref = self.buf.at[self.k.core, self.quarter, pl.ds(0, count), self.k.x]
             copy(ref, ref, self.z_s.at[0], self.z_r.at[0], self.k.z_device(1)).wait_recv()
 
         pl.when(self.sends)(lambda: got(self.zs - 1))
         pl.when(jnp.logical_not(self.sends))(lambda: got(self.zs))
-        for by in range(1, self.xs):
-            self.x_copy(by).start()
+        for way in BOTH:
+            self.over_x.start(way, 0)
+
+    def pass_x(self):
+        for way in BOTH:
+            self.over_x.step(1, way, 0)
 
     def collect(self):
-        self.x_all().wait_recv()
+        for way in BOTH:
+            self.over_x.step(2, way, 0)
         for chunk in range(2):
             self.first.start(1, chunk)
         for part in range(2):
-            self.hand(part, self.part_of(part, self.k.core, self.k.y)).start()
+            self.hand(part, self.part_of(part, self.k.core, self.quarter)).start()
 
     def up(self):
         for chunk in range(2):
@@ -381,12 +381,12 @@
         for part in range(2):
             self.all_of(part, self.k.core).wait_send()
 
-        self.x_all().wait_send()
+        self.over_x.finish()
 
         @pl.when(self.sends)
         def _():
-            ref = self.buf.at[self.k.core, pl.ds(0, self.k.z_count - 1), 0, self.k.x]
-            copy(ref, ref, self.z_s.at[0], self.z_r.at[0], self.k.z_device(1)).wait_send()
+            for by in range(1, self.k.z_count):
+                self.z_copy(by).wait_send()
 
 
 def kernel(
@@ -407,7 +407,7 @@
     count = (height // 2) * half_w
     width = keys.shape[2]
     wide = proj_all.shape[5]
-    per_half, narrow = qkv_all.shape[4:]
+    per_block, narrow = qkv_all.shape[4:]
     steps = z_count // 2
     plan = Plan()
 
@@ -432,10 +432,7 @@
         )
         for part in range(2)
     ]
-    piece = qkv.at[
-        pl.ds(pl.multiple_of(lax.div(k.y, 4) * per_half, 8), per_half),
-        pl.ds(pl.multiple_of(lax.rem(k.y, 4) * narrow, narrow), narrow),
-    ]
+    piece = qkv.at[:, pl.ds(pl.multiple_of(lax.rem(k.y, 4) * narrow, narrow), narrow)]
     proj_w = Proj(k, proj_all, proj_sems)
     qkv_w = Qkv(k, piece, qkv_all, qkv_sems)
     for one in quarters:
@@ -513,19 +510,20 @@
             plan.expect(8.8 + 1.8 * (2 * n - 1 + chunk), "b", functools.partial(proj_w.b_step, n, chunk))
     plan.expect(7.1 + 2.7 * steps, "a", proj_w.a_near)
     plan.expect(10.0 + 2.7 * steps, "a far", proj_w.a_far)
-    plan.expect(10.6, "collect", qkv_w.collect)
+    plan.expect(10.3, "qkv x", qkv_w.pass_x)
+    plan.expect(13.0, "collect", qkv_w.collect)
     plan.expect(12.0, "z", over_z.wait)
     for g in range(groups):
         for frame in range(frames):
             plan.expect(10.0 + 3.65 * g + 0.05 * frame, f"halo{g}", halo_copy(frame, g).wait_recv)
-    plan.expect(10.2 + 3.65 * (groups - 1), "up", qkv_w.up)
-    qkv_done = 12.6
+    plan.expect(16.5, "up", qkv_w.up)
+    qkv_done = 0.0
     for step, way, chunk in qkv_w.first.each():
-        time = (12.6 if way else 12.2 + 3.65 * (groups - 1)) + 1.7 * (2 * step - 1 + chunk)
+        time = (15.0 if way else 18.5) + 3.2 * (2 * step - 1 + chunk)
         qkv_done = max(qkv_done, time)
         plan.expect(time, "qkv", functools.partial(qkv_w.first.step, step, way, chunk))
     plan.expect(qkv_done + 0.1, "rest", qkv_w.rest)
-    plan.expect(qkv_done + 3.6, "qkv", functools.partial(qkv_w.wait, 0))
+    plan.expect(qkv_done + 1.7, "qkv", functools.partial(qkv_w.wait, 0))
     for step, way, chunk in qkv_w.last.each():
         plan.expect(qkv_done + 5.0 + 2.5 * step, "qkv last", functools.partial(qkv_w.last.step, step, way, chunk))
     plan.expect(qkv_done + 7.0 + 2.5 * max(qkv_w.last.reach), "qkv last", functools.partial(qkv_w.wait, 1))
@@ -696,16 +694,13 @@
         return mean, rsqrt(spread_sums[1:2] / token_count - mean * mean)
 
     def columns_of(block):
-        lanes = []
-        for lane_at in range(4):
-            chunks = []
-            for at in range(block * width // per_half, (block + 1) * width // per_half + 1):
-                owner, part = at // 2, at % 2
-                if owner < rows_count:
-                    own_z, own_x = owner // X, owner % X
-                    chunks.append(qkv_all[own_z % 2, 4 * part + lane_at, own_z // 2, own_x])
-            skip = block * width - block * width // per_half * per_half
-            lanes.append(jnp.concatenate(chunks, axis=0)[skip : skip + width])
+        first = block * width // per_block
+        owners = range(first, min(rows_count, (block + 1) * width // per_block + 1))
+        skip = block * width - first * per_block
+        lanes = [
+            jnp.concatenate([qkv_all[at // X % 2, quarter, at // X // 2, at % X] for at in owners], axis=0)[skip : skip + width]
+            for quarter in range(4)
+        ]
         return split(jnp.concatenate(lanes, axis=1))
 
     def query_key_weight():
@@ -859,15 +854,14 @@
     count = half_h * half_w
     steps = z_count // 2
     rows_count = z_count * X
-    proj_rows, qkv_rows = proj_weight.shape[1], qkv_weight.shape[1] // 2
+    proj_rows, qkv_rows = proj_weight.shape[1], qkv_weight.shape[1]
     wide, narrow = proj_weight.shape[0] // 4, qkv_weight.shape[0] // 4
-    y_count = tm_count // 2
-    far = y_count - 1 - (y_count - 1) // 3
+    far = 2
     vmem = pltpu.VMEM
     dma = pltpu.SemaphoreType.DMA
     proj_sems = [dma((2, steps)), dma((2, steps)), dma((3, z_count)), dma((3, z_count)), dma((X,)), dma((X,)), dma((4, steps)),
                  dma((4, steps)), dma((2,)), dma((2,))]
-    qkv_sems = [dma((1,)), dma((1,)), dma((1,)), dma((1,)), dma((1,)), dma((4, far)), dma((4, far)), dma((2, far)),
+    qkv_sems = [dma((1,)), dma((2, X // 2)), dma((2, X // 2)), dma((z_count,)), dma((1,)), dma((4, far)), dma((4, far)), dma((2, far)),
                 dma((2, far)), dma((2,)), dma((2,))]
     scratch = [
         vmem((2, frames, height, columns, 128), f32), vmem((2, frames, height, columns, 128), f32),
@@ -875,7 +869,7 @@
         vmem((X, tm_count, 128), f32), vmem((z_count, tm_count, 128), f32), vmem((tm_count, 1, 128), f32),
         vmem((X, 1, 128), f32), vmem((z_count, 1, 128), f32),
         vmem((2, 2, z_count, X, proj_rows, wide), f32),
-        vmem((2, y_count, z_count // 2, X, qkv_rows, narrow), f32),
+        vmem((2, 4, z_count // 2, X, qkv_rows, narrow), f32),
         vmem((4, 2 * half_h, 2 * half_w, channels), bf16), vmem((4, 2 * half_h, 2 * half_w, channels), bf16),
         vmem((frames, 2 * half_h, 2 * half_w, channels), f32),
         vmem((4, count, wide), bf16), vmem((4, count, wide), bf16),

time: 86.2 us -> 83.3 us (0.966); the launches traced: 86 us -> 82.1 us
  Pallas kernels: 84.2 us -> 80.3 us
    pallas_call x1, Pallas kernels: 84.2 us -> 80.3 us  [shards(): pl.pallas_call(functools.partial(kernel, z_count, tm_count), out_shape=(g...]
where the time goes in v8:
time: 83.3 us; the launch traced here: 82.1 us
  Pallas kernels  80.3 us (96%)
  other arithmetic  1.77 us (2%)
    pallas_call x1, Pallas kernels, shards(): pl.pallas_call(functools.partial(kernel, z_count, tm_count), out_shape=(g...  80.3 us
    add x1, other arithmetic, shards(): return tokens + attended  1.77 us

profile of v8, /device:TPU:6, one launch (start us, length us, event | category | flops | bytes accessed | tf_op | source)
XLA Modules:
  0.0 82.1 jit_solution(10755872850439339214)
XLA Ops:
  0.0 80.3 %shard_map.73 = (f32[1,2,64,512]{3,2,1,0:T(8,128)}, f32[1,2,64,512]{3,2,1,0:T(8,128)}) custom-call(f32[2,4,128,256]{3,2,1,0:T(8,128)} %features.1, f32[1,256]{1,0:T(1,128)} %bitcast.7, f32[3,256,256]{2,1,0:T(8,128)} %conv.1, f32[16,2048]{1,0:T(8,128)} %bitcast.4, f32[1,512]{1,0:T(1,128)} %bitcast.6, f32[48,512]{1,0:T(8,128)} %bitcast.5, f32[512,512]{1,0:T(8,128)} %out_weight.1), custom_call_target="tpu_custom_call" | custom-call | tf_op jit(solution)/shard_map/pallas_call | solution.py:892
  80.3 1.8 %add.3 = f32[1,2,64,512]{3,2,1,0:T(8,128)} add(f32[1,2,64,512]{3,2,1,0:T(8,128)} %get-tuple-element.7, f32[1,2,64,512]{3,2,1,0:T(8,128)} %get-tuple-element.8) | non-fusion elementwise | flops 65536 | bytes 786432 | tf_op jit(solution)/shard_map/add | solution.py:900

commit v9 on v8

--- a/solution.py
+++ b/solution.py
@@ -15,6 +15,7 @@
 NN = (((1,), (0,)), ((), ()))
 NT = (((1,), (1,)), ((), ()))
 BOTH = (0, 1)
+SLOWER = 1.4
 
 
 def split(value):
@@ -85,7 +86,7 @@
             self.need(name)
         self.upto(self.now)
         result = action()
-        self.now += duration
+        self.now += SLOWER * duration
         return result
 
 

time: 83.3 us -> 83.3 us (level); the launches traced: 82.1 us -> 83 us
  Pallas kernels: 80.3 us -> 81.3 us
    pallas_call x1, Pallas kernels: 80.3 us -> 81.3 us  [shards(): pl.pallas_call(functools.partial(kernel, z_count, tm_count), out_shape=(g...]
where the time goes in v9:
time: 83.3 us; the launch traced here: 83 us
  Pallas kernels  81.3 us (98%)
  other arithmetic  1.77 us (2%)
    pallas_call x1, Pallas kernels, shards(): pl.pallas_call(functools.partial(kernel, z_count, tm_count), out_shape=(g...  81.3 us
    add x1, other arithmetic, shards(): return tokens + attended  1.77 us

profile of v9, /device:TPU:6, one launch (start us, length us, event | category | flops | bytes accessed | tf_op | source)
XLA Modules:
  0.0 83.0 jit_solution(16752015066884717510)
XLA Ops:
  0.0 81.3 %shard_map.73 = (f32[1,2,64,512]{3,2,1,0:T(8,128)}, f32[1,2,64,512]{3,2,1,0:T(8,128)}) custom-call(f32[2,4,128,256]{3,2,1,0:T(8,128)} %features.1, f32[1,256]{1,0:T(1,128)} %bitcast.7, f32[3,256,256]{2,1,0:T(8,128)} %conv.1, f32[16,2048]{1,0:T(8,128)} %bitcast.4, f32[1,512]{1,0:T(1,128)} %bitcast.6, f32[48,512]{1,0:T(8,128)} %bitcast.5, f32[512,512]{1,0:T(8,128)} %out_weight.1), custom_call_target="tpu_custom_call" | custom-call | tf_op jit(solution)/shard_map/pallas_call | solution.py:893
  81.3 1.8 %add.3 = f32[1,2,64,512]{3,2,1,0:T(8,128)} add(f32[1,2,64,512]{3,2,1,0:T(8,128)} %get-tuple-element.7, f32[1,2,64,512]{3,2,1,0:T(8,128)} %get-tuple-element.8) | non-fusion elementwise | flops 65536 | bytes 786432 | tf_op jit(solution)/shard_map/add | solution.py:901
